TPU v7x, 32 devices: a whole 2x2x4 slice. The times are simulated.
32 devices in a mesh: grp: 2 (over y), seq: 8 (over z, x), lat: 2 (over core).
Axes of the slice: x: 2, y: 2, z: 4, core: 2. Of those that a mesh axis runs over, the one named last changes fastest.
Arguments:
- codes_idx: int32 [2048, 32], P(('grp', 'seq')), parts along dimension 0, may hold values from 0 to 65535, as said below
- codes_val: bfloat16 [2048, 32], P(('grp', 'seq')), parts along dimension 0, may hold values from 0.25 to 4
- decoder: bfloat16 [16, 16384, 2048], P(('seq', 'lat')), may hold values from -1 to 1
- decoder_offset_bias: bfloat16 [8192], P(('seq', 'lat')), may hold values from -3 to 3
- norm_gain: bfloat16 [8192], P(('seq', 'lat')), may hold values from 0.25 to 1.75
- w_query: bfloat16 [8192, 1024], P(('seq', 'lat')), may hold values from -0.09375 to 0.09375
- w_key: bfloat16 [8192, 128], P(('seq', 'lat')), may hold values from -0.09375 to 0.09375
- orig_queries: bfloat16 [8, 2048, 128], P('lat', ('grp', 'seq')), parts along dimension 1, may hold values from -40 to 40
- orig_keys: bfloat16 [2048, 128], P(('grp', 'seq')), parts along dimension 0, may hold values from -2.8 to 2.8
- mask_layout: int32 [16, 3], P('grp'), parts along dimension 0, may hold values from 0 to 1, as said below
Outputs:
- grad_vals: float32 [2048, 32], P(('grp', 'seq')), parts along dimension 0
There are 2 independent parts, one for each index of `grp`. A program takes and returns all parts, laid end to end along the dimension named above; an argument that names none is the same for every part. Nothing has to cross between parts.
Inputs may be any that keep to these rules, and one draw needn't show every extreme that they name: `codes_idx`: the 32 latents of a token are distinct. `mask_layout`: the last column is 1 in every row.
All inputs are finite; a program needn't handle non-finite values.
Results may differ from a plain program's by a relative error of at most 0.023.
Values may be sent and summed in bfloat16 or wider, within the bound.
A program may use at most 384 MiB of HBM per device.

v0:
```python
import math

import jax
import jax.numpy as jnp
from jax import lax
from jax.sharding import PartitionSpec as P

KL_WEIGHT = 16.0
EPSILON = 1e-05


def passed_along(array, axis, by):
    devices = lax.axis_size(axis)
    pairs = [(i, i + by) for i in range(devices) if 0 <= i + by < devices]
    return lax.ppermute(array, axis, pairs)


def decode_rows(decoder, all_idx, every_code_value, decoder_offset_bias):
    tokens, top_count = all_idx.shape
    step_rows = math.gcd(tokens, 1024)
    idx_blocks = all_idx.reshape(tokens // step_rows, step_rows, top_count)
    val_blocks = every_code_value.reshape(tokens // step_rows, step_rows, top_count)

    def decode_one_block(index_value_pair):
        decoder_weight_rows = jnp.take(decoder, index_value_pair[0], axis=0)
        return jnp.einsum(
            "bk,bkc->bc",
            index_value_pair[1],
            decoder_weight_rows,
            preferred_element_type=jnp.float32,
        )

    summed = lax.map(decode_one_block, (idx_blocks, val_blocks)).reshape(tokens, decoder.shape[1])
    return summed + decoder_offset_bias.astype(jnp.float32)[None, :]


def code_grads(decoder, all_idx, resid_grad):
    tokens, top_count = all_idx.shape
    step_rows = math.gcd(tokens, 1024)
    idx_blocks = all_idx.reshape(tokens // step_rows, step_rows, top_count)
    grad_blocks = resid_grad.reshape(tokens // step_rows, step_rows, resid_grad.shape[1])

    def code_one_block(index_gradient_pair):
        decoder_weight_rows = jnp.take(decoder, index_gradient_pair[0], axis=0)
        upper = lax.optimization_barrier(index_gradient_pair[1].astype(jnp.bfloat16))
        lower = (index_gradient_pair[1] - upper.astype(jnp.float32)).astype(jnp.bfloat16)
        first = jnp.einsum(
            "bc,bkc->bk", upper, decoder_weight_rows, preferred_element_type=jnp.float32
        )
        second_member = jnp.einsum(
            "bc,bkc->bk", lower, decoder_weight_rows, preferred_element_type=jnp.float32
        )
        return first + second_member

    return lax.map(code_one_block, (idx_blocks, grad_blocks)).reshape(tokens, top_count)


def attend(query_new, query_old, keys_new, keys_old, mask_layout, first_pos, block_len):
    range_len = query_new.shape[0]
    band_blocks = mask_layout.shape[1] - 1
    score_scale = 1.0 / math.sqrt(query_new.shape[1])
    query_at = first_pos + jnp.arange(range_len, dtype=jnp.int32)
    key_at = first_pos - range_len + jnp.arange(2 * range_len, dtype=jnp.int32)
    query_block = jnp.floor_divide(query_at, block_len)
    key_block = jnp.floor_divide(key_at, block_len)
    rel_slot = key_block[None, :] - query_block[:, None] + band_blocks
    layout_rows = lax.dynamic_slice_in_dim(
        mask_layout, first_pos // block_len, range_len // block_len, 0
    )
    layout_rows = jnp.repeat(layout_rows, block_len, axis=0)
    slot_ids = jnp.arange(band_blocks + 1, dtype=jnp.int32)
    layout_bit = jnp.sum(
        jnp.where(rel_slot[:, :, None] == slot_ids[None, None, :], layout_rows[:, None, :], 0),
        axis=2,
    )
    visible = (layout_bit > 0) & (key_block[None, :] >= 0) & (key_at[None, :] <= query_at[:, None])

    def softmax_rows(query_side, key_side):
        scores = (
            jnp.einsum("qe,ke->qk", query_side, key_side, preferred_element_type=jnp.float32)
            * score_scale
        )
        scores = jnp.where(visible, scores, -jnp.inf)
        row_max = jnp.max(scores, axis=1, keepdims=True)
        exp_scores = jnp.exp(scores - row_max)
        return exp_scores / jnp.sum(exp_scores, axis=1, keepdims=True)

    new_probs = softmax_rows(query_new, keys_new)
    old_probs = softmax_rows(query_old, keys_old)
    score_grad = (KL_WEIGHT * score_scale * (new_probs - old_probs)).astype(jnp.bfloat16)
    query_grad = jnp.einsum("qk,ke->qe", score_grad, keys_new, preferred_element_type=jnp.float32)
    key_gradient = jnp.einsum(
        "qk,qe->ke", score_grad, query_new, preferred_element_type=jnp.float32
    )
    return (query_grad.astype(jnp.bfloat16), key_gradient[:range_len], key_gradient[range_len:])


def local(
    codes_idx,
    codes_val,
    decoder,
    decoder_offset_bias,
    norm_gain,
    w_query,
    w_key,
    orig_queries,
    orig_keys,
    mask_layout,
):
    seq_count = lax.axis_size("seq")
    seq_index = lax.axis_index("seq")
    tok_rows = codes_idx.shape[0]
    heads_here = orig_queries.shape[0]
    head_dim = orig_keys.shape[1]
    all_heads = w_query.shape[1] // head_dim
    model_width = decoder_offset_bias.shape[0] * seq_count * lax.axis_size("lat")
    ranges = seq_count // heads_here
    range_len = tok_rows * heads_here
    block_len = tok_rows * seq_count // mask_layout.shape[0]
    flat_shape = (heads_here * tok_rows, head_dim)
    dec_local = decoder.reshape(decoder.shape[1] * 4, decoder_offset_bias.shape[0])
    all_idx, every_code_value = (
        lax.all_gather(codes_idx, "seq", axis=0, tiled=True),
        lax.all_gather(codes_val, "seq", axis=0, tiled=True),
    )
    residual = decode_rows(dec_local, all_idx, every_code_value, decoder_offset_bias).astype(
        jnp.bfloat16
    )
    resid_f32 = residual.astype(jnp.float32)
    squares = lax.psum(jnp.sum(resid_f32 * resid_f32, axis=1), ("seq", "lat"))
    inv_rms = lax.rsqrt(squares / model_width + EPSILON)
    gain_f32 = norm_gain.astype(jnp.float32)
    normed = (resid_f32 * inv_rms[:, None] * gain_f32[None, :]).astype(jnp.bfloat16)
    local_rows = lax.all_to_all(normed, "seq", split_axis=0, concat_axis=1, tiled=True)
    wq_rows, wk_rows = (
        lax.all_gather(w_query, "seq", axis=0, tiled=True),
        lax.all_gather(w_key, "seq", axis=0, tiled=True),
    )
    wq_heads = wq_rows.reshape(wq_rows.shape[0], all_heads, head_dim)
    query_part = jnp.einsum("td,dhe->hte", local_rows, wq_heads, preferred_element_type=jnp.float32)
    key_part = jnp.dot(local_rows, wk_rows, preferred_element_type=jnp.float32)
    query_mine = lax.psum_scatter(query_part, "lat", scatter_dimension=0, tiled=True)
    key_full = lax.psum(key_part, "lat")
    query_send = query_mine.astype(jnp.bfloat16).reshape(flat_shape)
    old_send = orig_queries.reshape(flat_shape)
    key_many = jnp.broadcast_to(
        key_full.astype(jnp.bfloat16)[None], (heads_here, tok_rows, head_dim)
    )
    old_many = jnp.broadcast_to(orig_keys[None], (heads_here, tok_rows, head_dim))
    first_pos = seq_index % ranges * range_len
    query_new, query_old, keys_new, keys_old = (
        lax.all_to_all(query_send, "seq", split_axis=0, concat_axis=0, tiled=True),
        lax.all_to_all(old_send, "seq", split_axis=0, concat_axis=0, tiled=True),
        lax.all_to_all(
            key_many.reshape(flat_shape), "seq", split_axis=0, concat_axis=0, tiled=True
        ),
        lax.all_to_all(
            old_many.reshape(flat_shape), "seq", split_axis=0, concat_axis=0, tiled=True
        ),
    )
    prev_new, prev_old = passed_along((keys_new, keys_old), "seq", 1)
    query_grad, key_grad_prev, key_grad_own = attend(
        query_new,
        query_old,
        jnp.concatenate([prev_new, keys_new], axis=0),
        jnp.concatenate([prev_old, keys_old], axis=0),
        mask_layout,
        first_pos,
        block_len,
    )
    query_grad_wide = query_grad.astype(jnp.float32)
    key_next = passed_along(key_grad_prev.astype(jnp.bfloat16), "seq", -1).astype(
        key_grad_prev.dtype
    )
    query_back, key_back = (
        lax.all_to_all(
            query_grad_wide.astype(jnp.bfloat16), "seq", split_axis=0, concat_axis=0, tiled=True
        ).astype(query_grad_wide.dtype),
        lax.all_to_all(
            (key_grad_own + key_next).astype(jnp.bfloat16),
            "seq",
            split_axis=0,
            concat_axis=0,
            tiled=True,
        ).astype(jnp.float32),
    )
    key_local = jnp.sum(key_back.reshape(heads_here, tok_rows, head_dim), axis=0)
    key_total = lax.psum(key_local.astype(jnp.bfloat16), "lat")
    query_heads_grad = query_back.astype(jnp.bfloat16).reshape(heads_here, tok_rows, head_dim)
    query_all = lax.all_gather(query_heads_grad, "lat", axis=0, tiled=True)
    normed_grad = jnp.einsum("hte,dhe->td", query_all, wq_heads, preferred_element_type=jnp.float32)
    normed_grad = normed_grad + jnp.einsum(
        "te,de->td", key_total, wk_rows, preferred_element_type=jnp.float32
    )
    normed_grad = normed_grad.astype(jnp.bfloat16)
    grad_cols = lax.all_to_all(normed_grad, "seq", split_axis=1, concat_axis=0, tiled=True).astype(
        jnp.float32
    )
    inner_sum = lax.psum(jnp.sum(grad_cols * gain_f32[None, :] * resid_f32, axis=1), ("seq", "lat"))
    resid_grad = (
        gain_f32[None, :] * inv_rms[:, None] * grad_cols
        - resid_f32 * (inv_rms * inv_rms * inv_rms * inner_sum / model_width)[:, None]
    )
    grad_part = code_grads(dec_local, all_idx, resid_grad)
    grad_seq = lax.psum_scatter(grad_part, "seq", scatter_dimension=0, tiled=True)
    return lax.psum(grad_seq, "lat")


def solution(mesh):
    in_specs = (
        P(("grp", "seq"), None),
        P(("grp", "seq"), None),
        P(("seq", "lat"), None, None),
        P(("seq", "lat")),
        P(("seq", "lat")),
        P(("seq", "lat"), None),
        P(("seq", "lat"), None),
        P("lat", ("grp", "seq"), None),
        P(("grp", "seq"), None),
        P("grp", None),
    )
    out_specs = P(("grp", "seq"), None)
    return jax.shard_map(local, mesh=mesh, in_specs=in_specs, out_specs=out_specs, check_vma=False)
```

profile of v0, /device:TPU:0, one launch (start us, length us, event | category | flops | bytes accessed | tf_op | source)
XLA Modules:
  0.0 1041.0 jit_solution(5450764328224032951)
XLA Ops:
  6.5 2.3 copy.35
  8.9 103.5 %reshape.169 = bf16[65536,512]{1,0:T(8,128)(2,1)} reshape(bf16[1,16384,2048]{2,1,0:T(8,128)(2,1)} %param.14) | data formatting | bytes 134217728 | tf_op jit(solution)/shard_map/reshape | solution.py:121
  112.4 35.8 %all_gather.15 = s32[1024,32]{0,1:T(8,128)S(1)} all-gather(s32[128,32]{0,1:T(8,128)S(1)} %copy-done.12), channel_id=1, replica_groups=mesh['grp'=2,'seq'=8,'lat'=2] {'seq'}, dimensions={0}, use_global_device_ids=true | all-gather | bytes 147456 | tf_op jit(solution)/shard_map/all_gather | solution.py:123
  148.9 26.0 %all_gather.16 = bf16[1024,32]{0,1:T(8,128)(2,1)S(1)} all-gather(bf16[128,32]{0,1:T(8,128)(2,1)S(1)} %copy-done.14), channel_id=1, replica_groups=mesh['grp'=2,'seq'=8,'lat'=2] {'seq'}, dimensions={0}, use_global_device_ids=true | all-gather | bytes 73728 | tf_op jit(solution)/shard_map/all_gather | solution.py:124
  174.9 0.4 copy.40
  175.3 530.6 %gather_fusion = bf16[32768,512]{1,0:T(8,128)(2,1)} fusion(bf16[65536,512]{1,0:T(8,128)(2,1)} %reshape.169, s32[32768]{0:T(1024)S(1)} %broadcast_clamp_fusion), kind=kCustom, calls=%fused_computation.clone | custom fusion | bytes 67239936 | tf_op jit(solution)/shard_map/while/body/eval_jaxpr/jit(_take)/gather | solution.py:25
  706.0 11.6 %fusion.2 = f32[1024,1,512]{2,1,0:T(1,128)S(1)} fusion(bf16[1024,32,1]{1,2,0:T(2,128)(2,1)S(1)} %copy.40, bf16[1024,32,512]{2,1,0:T(8,128)(2,1)} %bitcast.79, pred[1024,32]{1,0:T(8,128)(4,1)S(1)} %copy.32), kind=kOutput, calls=%fused_computation.4 | convolution fusion | flops 50331648 | bytes 35749888 | tf_op jit(solution)/shard_map/while/body/eval_jaxpr/bk,bkc->bc/dot_general | solution.py:26
  717.8 0.3 fusion.7
  718.1 29.5 %psum.35 = f32[1024]{0:T(1024)S(1)} all-reduce(f32[1024]{0:T(1024)S(1)} %get-tuple-element.24), channel_id=1, replica_groups=mesh['grp'=2,'seq'=8,'lat'=2] {'seq','lat'}, use_global_device_ids=true, to_apply=%region_1.3 | all-reduce | flops 1024 | bytes 8192 | tf_op jit(solution)/shard_map/psum | solution.py:130
  747.6 1.3 fusion.10
  748.9 3.7 all-to-all-start
  752.7 0.7 all-gather.5.cloned.1.call-update
  753.6 0.6 iota_add_fusion.1
  754.2 0.6 iota_add_fusion
  754.8 1.5 subtract_add_fusion
  756.3 26.5 %all-to-all-done = bf16[8,128,512]{2,1,0:T(8,128)(2,1)S(1)} async-done(((bf16[8,128,512]{2,1,0:T(8,128)(2,1)}), bf16[8,128,512]{2,1,0:T(8,128)(2,1)S(1)}, u32[]{:S(2)}, u32[]{:S(2)}) %all-to-all-start) | async-done | bytes 1048608 | tf_op jit(solution)/shard_map/all_to_all | solution.py:134
  782.8 0.7 broadcast_in_dim.45
  783.5 3.6 all-to-all-start.3
  787.2 1.6 copy.34
  788.7 1.6 reshape.190
  790.3 7.1 convolution_bitcast_fusion.1
  797.4 0.6 broadcast_compare_fusion
  798.0 3.5 select_reduce_fusion
  801.5 5.9 all-to-all-start.4
  807.4 4.6 collective-permute-start.1
  812.0 1.1 copy.50
  813.1 2.1 fusion.40
  815.2 3.6 psum.36
  818.9 0.7 broadcast_in_dim.43
  819.6 3.9 all-to-all-start.2
  823.5 2.1 compare_and_fusion
  825.5 1.6 convert_element_type.85
  827.2 3.8 all-to-all-done.2
  831.0 3.4 all-to-all-start.1
  834.3 1.8 fusion.38
  836.1 4.0 collective-permute-start
  840.1 1.1 fusion.16
  841.2 1.2 collective-permute-done
  842.4 1.6 fusion.39
  844.1 0.5 fusion.15
  844.6 1.2 multiply_convert_fusion
  845.8 0.5 fusion.41
  846.3 1.3 collective-permute-start.2
  847.6 1.1 convolution_convert_fusion
  848.7 8.5 all-to-all-start.5
  857.2 0.7 fusion.18
  857.9 6.7 all-to-all-done.5
  864.5 3.4 all-to-all-start.6
  868.0 2.0 all_gather.19
  869.9 4.7 convolution_bitcast_fusion
  874.7 0.5 all-to-all-done.6
  875.2 3.4 psum.37
  878.6 1.7 fusion.6
  880.4 31.5 %all_to_all.98 = bf16[128,8,512]{2,0,1:T(8,128)(2,1)S(1)} all-to-all(bf16[128,8,512]{2,0,1:T(8,128)(2,1)S(1)} %bitcast.89), channel_id=1, replica_groups=mesh['grp'=2,'seq'=8,'lat'=2] {'seq'}, dimensions={1} | all-to-all | bytes 2097152 | tf_op jit(solution)/shard_map/all_to_all | solution.py:196
  912.0 0.4 fusion.11
  912.4 31.4 %psum.38 = f32[1024]{0:T(1024)S(1)} all-reduce(f32[1024]{0:T(1024)S(1)} %bitcast.106), channel_id=1, replica_groups=mesh['grp'=2,'seq'=8,'lat'=2] {'seq','lat'}, use_global_device_ids=true, to_apply=%region_12.14 | all-reduce | flops 1024 | bytes 8192 | tf_op jit(solution)/shard_map/psum | solution.py:199
  943.8 0.5 fusion.17
  944.3 0.7 subtract_convert_fusion
  945.2 13.1 %fusion = f32[1024,1,32]{2,1,0:T(1,128)S(1)} fusion(bf16[1024,32,512]{2,1,0:T(8,128)(2,1)} %bitcast.80, pred[1024,32]{1,0:T(8,128)(4,1)S(1)} %copy-done.6, bf16[1024,512,1]{1,0,2:T(8,128)(2,1)S(1)} %bitcast.94), kind=kOutput, calls=%fused_computation.2 | convolution fusion | flops 50331648 | bytes 34766848 | tf_op jit(solution)/shard_map/while/body/eval_jaxpr/bc,bkc->bk/dot_general | solution.py:50
  958.6 13.0 %fusion.1 = f32[1024,1,32]{2,1,0:T(1,128)S(1)} fusion(bf16[1024,32,512]{2,1,0:T(8,128)(2,1)} %bitcast.81, pred[1024,32]{1,0:T(8,128)(4,1)S(1)} %copy-done.6, bf16[1024,512,1]{1,0,2:T(8,128)(2,1)S(1)} %bitcast.91), kind=kOutput, calls=%fused_computation.3 | convolution fusion | flops 50331648 | bytes 34766848 | tf_op jit(solution)/shard_map/while/body/eval_jaxpr/bc,bkc->bk/dot_general | solution.py:47
  971.6 0.3 copy.46
  971.9 0.7 bitcast_add_fusion.1
  972.6 57.3 %reduce-scatter.5.cloned.1.call-done = f32[128,32]{0,1:T(8,128)} async-done(((f32[1024,32]{0,1:T(8,128)}), f32[128,32]{0,1:T(8,128)}) %reduce-scatter.5.cloned.1.call-update) | async-done | bytes 16400 | tf_op jit(solution)/shard_map/reduce_scatter | solution.py:205
  1029.9 4.6 psum.39
  (69 shorter events, 2.0 us)
Async XLA Ops:
  6.5 746.9 %copy-start = (s32[8,3]{0,1:T(4,128)S(1)}, s32[8,3]{0,1:T(4,128)}, u32[]{:S(2)}) copy-start(s32[8,3]{0,1:T(4,128)} %param.21) | copy-start | bytes 292
  6.5 783.8 %all-gather.3.cloned.1.call-start = ((), (), s32[]{:S(2)}) async-start(), calls=%async_computation.10 | async-start | bytes 9437184 | tf_op jit(solution)/shard_map/all_gather | solution.py:136
  8.9 103.6 %copy-start.12 = (s32[128,32]{0,1:T(8,128)S(1)}, s32[128,32]{0,1:T(8,128)}, u32[]{:S(2)}) copy-start(s32[128,32]{0,1:T(8,128)} %param.12) | copy-start | bytes 49156
  8.9 140.0 %copy-start.15 = (bf16[512]{0:T(512)(128)(2,1)S(1)}, bf16[512]{0:T(512)(128)(2,1)}, u32[]{:S(2)}) copy-start(bf16[512]{0:T(512)(128)(2,1)} %param.15) | copy-start | bytes 3076
  8.9 140.0 %copy-start.14 = (bf16[128,32]{0,1:T(8,128)(2,1)S(1)}, bf16[128,32]{0,1:T(8,128)(2,1)}, u32[]{:S(2)}) copy-start(bf16[128,32]{0,1:T(8,128)(2,1)} %param.13) | copy-start | bytes 24580
  112.4 62.9 %copy-start.16 = (bf16[512]{0:T(512)(128)(2,1)S(1)}, bf16[512]{0:T(512)(128)(2,1)}, u32[]{:S(2)}) copy-start(bf16[512]{0:T(512)(128)(2,1)} %param.16) | copy-start | bytes 3076
  148.9 557.1 %copy-start.5 = (pred[1024,32]{1,0:T(8,128)(4,1)}, pred[1024,32]{1,0:T(8,128)(4,1)S(1)}, u32[]{:S(2)}) copy-start(pred[1024,32]{1,0:T(8,128)(4,1)S(1)} %copy.32) | copy-start | bytes 98308
  148.9 598.7 %copy-start.8 = (f32[512]{0:T(512)}, f32[512]{0:T(512)S(1)}, u32[]{:S(2)}) copy-start(f32[512]{0:T(512)S(1)} %convert_element_type.79) | copy-start | bytes 6148
  717.8 31.1 %copy-start.1 = (f32[1024,1,512]{2,0,1:T(8,128)}, f32[1024,1,512]{2,0,1:T(8,128)S(1)}, u32[]{:S(2)}) copy-start(f32[1024,1,512]{2,0,1:T(8,128)S(1)} %copy.41) | copy-start | bytes 6291460
  748.9 33.9 %copy-start.7 = (bf16[128,128]{1,0:T(8,128)(2,1)S(1)}, bf16[128,128]{1,0:T(8,128)(2,1)}, u32[]{:S(2)}) copy-start(bf16[128,128]{1,0:T(8,128)(2,1)} %param.20) | copy-start | bytes 98308
  748.9 33.9 %all-to-all-start = ((bf16[8,128,512]{2,1,0:T(8,128)(2,1)}), bf16[8,128,512]{2,1,0:T(8,128)(2,1)S(1)}, u32[]{:S(2)}, u32[]{:S(2)}) async-start(bf16[8,128,512]{2,1,0:T(8,128)(2,1)} %fusion.10), calls=%async_computation | async-start | bytes 2097152 | tf_op jit(solution)/shard_map/all_to_all | solution.py:134
  752.6 60.5 %all-gather.5.cloned.1.call-start = ((), (), s32[]{:S(2)}) async-start(), calls=%async_computation.12 | async-start | bytes 1179648 | tf_op jit(solution)/shard_map/all_gather | solution.py:137
  783.5 18.0 %all-to-all-start.3 = ((bf16[8,64,128]{2,1,0:T(8,128)(2,1)}), bf16[8,64,128]{2,1,0:T(8,128)(2,1)S(1)}, u32[]{:S(2)}, u32[]{:S(2)}) async-start(bf16[8,64,128]{2,1,0:T(8,128)(2,1)} %bitcast.12), calls=%async_computation.4 | async-start | bytes 262144 | tf_op jit(solution)/shard_map/all_to_all | solution.py:157
  787.1 38.4 %reduce-scatter.3.cloned.1.call-start = ((), (), s32[]{:S(2)}) async-start(), calls=%async_computation.11 | async-start | bytes 786432 | tf_op jit(solution)/shard_map/reduce_scatter | solution.py:142
  801.5 17.4 %all-to-all-start.4 = ((bf16[8,64,128]{2,1,0:T(8,128)(2,1)}), bf16[8,64,128]{2,1,0:T(8,128)(2,1)S(1)}, u32[]{:S(2)}, u32[]{:S(2)}) async-start(bf16[8,64,128]{2,1,0:T(8,128)(2,1)} %bitcast.14), calls=%async_computation.5 | async-start | bytes 262144 | tf_op jit(solution)/shard_map/all_to_all | solution.py:153
  807.4 26.9 %collective-permute-start.1 = (bf16[512,128]{1,0:T(8,128)(2,1)S(1)}, bf16[512,128]{1,0:T(8,128)(2,1)}, u32[]{:S(2)}, u32[]{:S(2)}) collective-permute-start(bf16[512,128]{1,0:T(8,128)(2,1)S(1)} %bitcast.95), channel_id=1, source_target_pairs={{0,2},{2,4},{4,6},{6,8},{8,10},{10,12},{12,14},{1,3},{3,5},{5,7},{... | collective-permute-start | bytes 393224 | tf_op jit(solution)/shard_map/ppermute | solution.py:15
  813.1 10.4 copy-start.3
  818.9 12.1 %copy-start.4 = (bf16[8,64,128]{2,1,0:T(8,128)(2,1)}, bf16[8,64,128]{2,1,0:T(8,128)(2,1)S(1)}, u32[]{:S(2)}) copy-start(bf16[8,64,128]{2,1,0:T(8,128)(2,1)S(1)} %all-to-all-done.4) | copy-start | bytes 393220
  819.6 11.4 %all-to-all-start.2 = ((bf16[8,64,128]{2,1,0:T(8,128)(2,1)}), bf16[8,64,128]{2,1,0:T(8,128)(2,1)S(1)}, u32[]{:S(2)}, u32[]{:S(2)}) async-start(bf16[8,64,128]{2,1,0:T(8,128)(2,1)} %bitcast.102), calls=%async_computation.3 | async-start | bytes 262144 | tf_op jit(solution)/shard_map/all_to_all | solution.py:154
  831.0 11.5 %all-to-all-start.1 = ((bf16[8,64,128]{2,1,0:T(8,128)(2,1)}), bf16[8,64,128]{2,1,0:T(8,128)(2,1)S(1)}, u32[]{:S(2)}, u32[]{:S(2)}) async-start(bf16[8,64,128]{2,1,0:T(8,128)(2,1)} %bitcast.8), calls=%async_computation.2 | async-start | bytes 262144 | tf_op jit(solution)/shard_map/all_to_all | solution.py:152
  836.1 5.1 copy-start.10
  836.1 6.3 collective-permute-start
  842.4 2.2 copy-start.11
  842.4 2.2 copy-start.13
  846.3 10.9 %collective-permute-start.2 = (bf16[512,128]{1,0:T(8,128)(2,1)S(1)}, bf16[512,128]{1,0:T(8,128)(2,1)S(1)}, u32[]{:S(2)}, u32[]{:S(2)}) collective-permute-start(bf16[512,128]{1,0:T(8,128)(2,1)S(1)} %slice.17), channel_id=1, source_target_pairs={{2,0},{4,2},{6,4},{8,6},{10,8},{12,10},{14,12},{3,1},{5,3},{7,5},{... | collective-permute-start | bytes 393224 | tf_op jit(solution)/shard_map/ppermute | solution.py:15
  848.7 15.9 %all-to-all-start.5 = ((bf16[8,64,128]{2,1,0:T(8,128)(2,1)}), bf16[8,64,128]{2,1,0:T(8,128)(2,1)S(1)}, u32[]{:S(2)}, u32[]{:S(2)}) async-start(bf16[8,64,128]{2,1,0:T(8,128)(2,1)} %bitcast.17), calls=%async_computation.6 | async-start | bytes 262144 | tf_op jit(solution)/shard_map/all_to_all | solution.py:176
  864.5 10.7 %all-to-all-start.6 = ((bf16[8,64,128]{2,1,0:T(8,128)(2,1)}), bf16[8,64,128]{2,1,0:T(8,128)(2,1)S(1)}, u32[]{:S(2)}, u32[]{:S(2)}) async-start(bf16[8,64,128]{2,1,0:T(8,128)(2,1)} %bitcast.20), calls=%async_computation.7 | async-start | bytes 262144 | tf_op jit(solution)/shard_map/all_to_all | solution.py:179
  867.9 162.0 %reduce-scatter.5.cloned.1.call-start = ((), (), s32[]{:S(2)}) async-start(), calls=%async_computation.13 | async-start | bytes 147456 | tf_op jit(solution)/shard_map/reduce_scatter | solution.py:205
  880.3 31.6 %copy-start.2 = (f32[1024,1,512]{2,0,1:T(8,128)S(1)}, f32[1024,1,512]{2,0,1:T(8,128)}, u32[]{:S(2)}) copy-start(f32[1024,1,512]{2,0,1:T(8,128)} %copy-done.1) | copy-start | bytes 6291460
  880.3 31.6 %copy-start.9 = (f32[512]{0:T(512)S(1)}, f32[512]{0:T(512)}, u32[]{:S(2)}) copy-start(f32[512]{0:T(512)} %copy-done.8) | copy-start | bytes 6148
  944.3 0.9 copy-start.6
Sparse Core Ops, SparseCore 0:
  9.4 129.0 all-gather.2
  755.6 47.6 all-gather.4
  805.5 5.7 reduce-scatter.2
  972.7 57.0 reduce-scatter.4
where the time goes:
time: 1050 us; the launch traced here: 1040 us
  local copies, waits for them, and re-layouts  644 us (61%)
  blocking collectives  168 us (16%)
  waiting for transfers between devices  96.8 us (9%)
  matrix products  58.3 us (6%)
  starting transfers between devices  42.4 us (4%)
  other arithmetic  17.9 us (2%)
  between operations  13.6 us (1%)
    gather x1, local copies, waits for them, and re-layouts, decode_one_block(): decoder_weight_rows = jnp.take(decoder, index_value_pair[0], axis=0)  531 us
    reshape x1, local copies, waits for them, and re-layouts, local(): decoder.reshape(decoder.shape[1] * 4, decoder_offset_bias.shape[0])  104 us
    reduce_scatter x1, waiting for transfers between devices, local(): lax.psum_scatter(grad_part, 'seq', scatter_dimension=0, tiled=True)  57.3 us
    all_gather x1, blocking collectives, local(): lax.all_gather(codes_idx, 'seq', axis=0, tiled=True)  35.8 us
    all_to_all x1, blocking collectives, local(): lax.all_to_all(normed_grad, 'seq', split_axis=1, concat_axis=0, tiled=True)  31.5 us
    psum x1, blocking collectives, local(): lax.psum(jnp.sum(grad_cols * gain_f32[None, :] * resid_f32, axis=1), ('se...  31.4 us
    psum x1, blocking collectives, local(): squares = lax.psum(jnp.sum(resid_f32 * resid_f32, axis=1), ('seq', 'lat'))  29.5 us
    all_to_all x1, waiting for transfers between devices, local(): lax.all_to_all(normed, 'seq', split_axis=0, concat_axis=1, tiled=True)  26.5 us
  transfers between devices with their start and end apart: 14, of which 6 were waited for; matrix products, arithmetic and copies ran while one was open for 66% of the time, Pallas kernels for 0%

commit v1 on v0

--- a/solution.py
+++ b/solution.py
@@ -3,6 +3,8 @@
 import jax
 import jax.numpy as jnp
 from jax import lax
+from jax.experimental import pallas as pl
+from jax.experimental.pallas import tpu as pltpu
 from jax.sharding import PartitionSpec as P
 
 KL_WEIGHT = 16.0
@@ -13,6 +15,76 @@
     devices = lax.axis_size(axis)
     pairs = [(i, i + by) for i in range(devices) if 0 <= i + by < devices]
     return lax.ppermute(array, axis, pairs)
+
+
+LATENTS_PER_ROW = 4
+LANES = 128
+PAIR_BLOCK = 2048
+CONVERT_ROWS = 256
+UNROLL = 32
+
+
+def gather_kernel(idx_ref, block_ref, out_ref, table, picked):
+    step = pl.program_id(1)
+    rows = block_ref.shape[0]
+
+    @pl.when(step < LATENTS_PER_ROW)
+    def _():
+        def convert(i, carry):
+            at = pl.multiple_of(i * CONVERT_ROWS, CONVERT_ROWS)
+            table[pl.ds(step * rows + at, CONVERT_ROWS), :] = block_ref[
+                pl.ds(at, CONVERT_ROWS), :
+            ].astype(jnp.float32)
+            return carry
+
+        lax.fori_loop(0, rows // CONVERT_ROWS, convert, 0)
+
+    @pl.when(step >= LATENTS_PER_ROW)
+    def _():
+        first = (step - LATENTS_PER_ROW) * PAIR_BLOCK
+
+        def pick(i, carry):
+            at = pl.multiple_of(i * UNROLL, UNROLL)
+            loaded = [table[pl.ds(idx_ref[first + at + k], 1), :] for k in range(UNROLL)]
+            for k in range(UNROLL):
+                picked[pl.ds(at + k, 1), :] = loaded[k]
+            return carry
+
+        lax.fori_loop(0, PAIR_BLOCK // UNROLL, pick, 0)
+        out_ref[...] = picked[...].astype(out_ref.dtype)
+
+
+def gather_rows(decoder, all_idx):
+    rows, wide = decoder.shape
+    features = wide // LATENTS_PER_ROW
+    parts = features // LANES
+    pairs = all_idx.size
+    flat = all_idx.reshape(pairs)
+    table_row = (flat % LATENTS_PER_ROW) * rows + flat // LATENTS_PER_ROW
+
+    def in_block(part, step, idx_ref):
+        loading = step < LATENTS_PER_ROW
+        following = jnp.minimum(part + 1, parts - 1)
+        return (0, jnp.where(loading, step * parts + part, following))
+
+    def out_block(part, step, idx_ref):
+        return (jnp.maximum(step - LATENTS_PER_ROW, 0), part)
+
+    return pl.pallas_call(
+        gather_kernel,
+        out_shape=jax.ShapeDtypeStruct((pairs, features), decoder.dtype),
+        grid_spec=pltpu.PrefetchScalarGridSpec(
+            num_scalar_prefetch=1,
+            grid=(parts, LATENTS_PER_ROW + pairs // PAIR_BLOCK),
+            in_specs=[pl.BlockSpec((rows, LANES), in_block)],
+            out_specs=pl.BlockSpec((PAIR_BLOCK, LANES), out_block),
+            scratch_shapes=[
+                pltpu.VMEM((LATENTS_PER_ROW * rows, LANES), jnp.float32),
+                pltpu.VMEM((PAIR_BLOCK, LANES), jnp.float32),
+            ],
+        ),
+        compiler_params=pltpu.CompilerParams(vmem_limit_bytes=52 * 1024 * 1024),
+    )(table_row, decoder)
 
 
 def decode_rows(decoder, all_idx, every_code_value, decoder_offset_bias):
@@ -118,14 +190,22 @@
     range_len = tok_rows * heads_here
     block_len = tok_rows * seq_count // mask_layout.shape[0]
     flat_shape = (heads_here * tok_rows, head_dim)
-    dec_local = decoder.reshape(decoder.shape[1] * 4, decoder_offset_bias.shape[0])
     all_idx, every_code_value = (
         lax.all_gather(codes_idx, "seq", axis=0, tiled=True),
         lax.all_gather(codes_val, "seq", axis=0, tiled=True),
     )
-    residual = decode_rows(dec_local, all_idx, every_code_value, decoder_offset_bias).astype(
-        jnp.bfloat16
-    )
+    features = decoder_offset_bias.shape[0]
+    picked_rows = None
+    if features % LANES == 0:
+        picked_rows = gather_rows(decoder[0], all_idx).reshape(*all_idx.shape, features)
+        residual = jnp.einsum(
+            "bk,bkc->bc", every_code_value, picked_rows, preferred_element_type=jnp.float32
+        )
+        residual = residual + decoder_offset_bias.astype(jnp.float32)[None, :]
+    else:
+        dec_local = decoder.reshape(decoder.shape[1] * LATENTS_PER_ROW, features)
+        residual = decode_rows(dec_local, all_idx, every_code_value, decoder_offset_bias)
+    residual = residual.astype(jnp.bfloat16)
     resid_f32 = residual.astype(jnp.float32)
     squares = lax.psum(jnp.sum(resid_f32 * resid_f32, axis=1), ("seq", "lat"))
     inv_rms = lax.rsqrt(squares / model_width + EPSILON)
@@ -201,7 +281,15 @@
         gain_f32[None, :] * inv_rms[:, None] * grad_cols
         - resid_f32 * (inv_rms * inv_rms * inv_rms * inner_sum / model_width)[:, None]
     )
-    grad_part = code_grads(dec_local, all_idx, resid_grad)
+    if picked_rows is not None:
+        grad_part = jnp.einsum(
+            "bc,bkc->bk",
+            resid_grad.astype(jnp.bfloat16),
+            picked_rows,
+            preferred_element_type=jnp.float32,
+        )
+    else:
+        grad_part = code_grads(dec_local, all_idx, resid_grad)
     grad_seq = lax.psum_scatter(grad_part, "seq", scatter_dimension=0, tiled=True)
     return lax.psum(grad_seq, "lat")
 

time: 1050 us -> 569 us (0.54)
  local copies, waits for them, and re-layouts: 644 us -> 9.77 us
  Pallas kernels: 0 us -> 171 us
    gather x1 -> x0, local copies, waits for them, and re-layouts: 531 us -> none  [decode_one_block(): decoder_weight_rows = jnp.take(decoder, index_value_pair[0], axis=0)]
    pallas_call x0 -> x1, Pallas kernels: none -> 171 us  [gather_rows(): pl.pallas_call(gather_kernel, out_shape=jax.ShapeDtypeStruct((pairs, feat...]
    reshape x1, local copies, waits for them, and re-layouts: 104 us -> 0.17 us  [gather_rows(): flat = all_idx.reshape(pairs)]
    dot_general x3 -> x2, matrix products: 37.8 us -> 28.6 us  [the longest x1 16.2 us: local(): jnp.einsum('bc,bkc->bk', resid_grad.astype(jnp.bfloat16), picked_rows, pr...]
  transfers between devices with their start and end apart: 14 -> 14, of which waited for: 6 -> 6; matrix products, arithmetic and copies ran while one was open for 66% -> 9% of each run, Pallas kernels for 0% -> 30%
where the time goes in v1:
time: 569 us; the launch traced here: 567 us
  Pallas kernels  171 us (30%)
  blocking collectives  166 us (29%)
  waiting for transfers between devices  99 us (17%)
  matrix products  49.2 us (9%)
  starting transfers between devices  42.5 us (7%)
  other arithmetic  16 us (3%)
  between operations  13.5 us (2%)
  local copies, waits for them, and re-layouts  9.77 us (2%)
    pallas_call x1, Pallas kernels, gather_rows(): pl.pallas_call(gather_kernel, out_shape=jax.ShapeDtypeStruct((pairs, feat...  171 us
    reduce_scatter x1, waiting for transfers between devices, local(): lax.psum_scatter(grad_part, 'seq', scatter_dimension=0, tiled=True)  59 us
    all_gather x1, blocking collectives, local(): lax.all_gather(codes_idx, 'seq', axis=0, tiled=True)  32.9 us
    all_to_all x1, blocking collectives, local(): lax.all_to_all(normed_grad, 'seq', split_axis=1, concat_axis=0, tiled=True)  31.4 us
    psum x1, blocking collectives, local(): lax.psum(jnp.sum(grad_cols * gain_f32[None, :] * resid_f32, axis=1), ('se...  31.4 us
    psum x1, blocking collectives, local(): squares = lax.psum(jnp.sum(resid_f32 * resid_f32, axis=1), ('seq', 'lat'))  29.5 us
    all_gather x1, blocking collectives, local(): lax.all_gather(codes_val, 'seq', axis=0, tiled=True)  27.1 us
    all_to_all x1, waiting for transfers between devices, local(): lax.all_to_all(normed, 'seq', split_axis=0, concat_axis=1, tiled=True)  27 us
  transfers between devices with their start and end apart: 14, of which 6 were waited for; matrix products, arithmetic and copies ran while one was open for 9% of the time, Pallas kernels for 30%

profile of v1, /device:TPU:0, one launch (start us, length us, event | category | flops | bytes accessed | tf_op | source)
XLA Modules:
  0.0 567.0 jit_solution(18341481375312777667)
XLA Ops:
  6.5 2.3 copy.31
  8.9 32.9 %all_gather.15 = s32[1024,32]{0,1:T(8,128)S(1)} all-gather(s32[128,32]{0,1:T(8,128)S(1)} %copy-done.5), channel_id=1, replica_groups=mesh['grp'=2,'seq'=8,'lat'=2] {'seq'}, dimensions={0}, use_global_device_ids=true | all-gather | bytes 147456 | tf_op jit(solution)/shard_map/all_gather | solution.py:194
  41.8 0.2 copy.29
  42.0 0.2 reshape.128
  42.1 27.1 %all_gather.16 = bf16[1024,32]{0,1:T(8,128)(2,1)S(1)} all-gather(bf16[128,32]{0,1:T(8,128)(2,1)S(1)} %copy-done.7), channel_id=1, replica_groups=mesh['grp'=2,'seq'=8,'lat'=2] {'seq'}, dimensions={0}, use_global_device_ids=true | all-gather | bytes 73728 | tf_op jit(solution)/shard_map/all_gather | solution.py:195
  69.3 0.4 copy.36
  69.7 0.1 fusion.17.idx_ref
  69.8 171.2 %shard_map.100 = bf16[32768,512]{1,0:T(8,128)(2,1)} custom-call(s32[32768]{0:T(1024)S(1)} %fusion.17.idx_ref, bf16[16384,2048]{1,0:T(8,128)(2,1)} %bitcast.block_ref), custom_call_target="tpu_custom_call" | custom-call | tf_op jit(solution)/shard_map/pallas_call | solution.py:73
  241.0 12.4 %fusion.36 = f32[1024,1,512]{2,1,0:T(1,128)S(1)} fusion(bf16[1024,32,512]{2,1,0:T(8,128)(2,1)} %bitcast.71, bf16[1024,32,1]{1,2,0:T(2,128)(2,1)S(1)} %copy.36), kind=kOutput, calls=%fused_computation.84 | convolution fusion | flops 33554432 | bytes 35717120 | tf_op jit(solution)/shard_map/bk,bkc->bc/dot_general | solution.py:201
  253.4 0.3 fusion.1
  253.7 29.5 %psum.35 = f32[1024]{0:T(1024)S(1)} all-reduce(f32[1024]{0:T(1024)S(1)} %get-tuple-element.5), channel_id=1, replica_groups=mesh['grp'=2,'seq'=8,'lat'=2] {'seq','lat'}, use_global_device_ids=true, to_apply=%region_1.2 | all-reduce | flops 1024 | bytes 8192 | tf_op jit(solution)/shard_map/psum | solution.py:210
  283.2 1.3 fusion.3
  284.5 3.7 all-to-all-start
  288.3 0.7 all-gather.5.cloned.1.call-update
  289.0 0.1 constant_dynamic-slice_fusion
  289.2 0.6 iota_add_fusion.1
  289.8 1.6 subtract_add_fusion
  291.4 27.0 %all-to-all-done = bf16[8,128,512]{2,1,0:T(8,128)(2,1)S(1)} async-done(((bf16[8,128,512]{2,1,0:T(8,128)(2,1)}), bf16[8,128,512]{2,1,0:T(8,128)(2,1)S(1)}, u32[]{:S(2)}, u32[]{:S(2)}) %all-to-all-start) | async-done | bytes 1048608 | tf_op jit(solution)/shard_map/all_to_all | solution.py:214
  318.4 0.7 broadcast_in_dim.31
  319.1 3.6 all-to-all-start.3
  322.8 1.5 copy.30
  324.3 1.6 reshape.135
  325.9 7.1 %convolution_bitcast_fusion.1 = f32[8,128,128]{2,1,0:T(8,128)} fusion(bf16[128,4096,1]{1,0,2:T(8,128)(2,1)S(1)} %reshape.135, bf16[4096,8,128]{0,2,1:T(8,128)(2,1)} %bitcast.73), kind=kOutput, calls=%fused_computation.30 | convolution fusion | flops 1073741824 | bytes 9961472 | tf_op jit(solution)/shard_map/td,dhe->hte/dot_general | solution.py:220
  333.0 0.6 broadcast_compare_fusion
  333.6 3.5 select_reduce_fusion
  337.1 6.0 %all-to-all-start.4 = ((bf16[8,64,128]{2,1,0:T(8,128)(2,1)}), bf16[8,64,128]{2,1,0:T(8,128)(2,1)S(1)}, u32[]{:S(2)}, u32[]{:S(2)}) async-start(bf16[8,64,128]{2,1,0:T(8,128)(2,1)} %bitcast.14), calls=%async_computation.5 | async-start | bytes 262144 | tf_op jit(solution)/shard_map/all_to_all | solution.py:233
  343.0 4.6 collective-permute-start.1
  347.6 1.1 copy.44
  348.7 2.1 fusion.37
  350.8 3.6 psum.36
  354.4 0.7 broadcast_in_dim.29
  355.1 4.0 all-to-all-start.2
  359.1 2.1 compare_and_fusion
  361.2 1.6 convert_element_type.61
  362.8 3.8 all-to-all-done.2
  366.6 3.4 all-to-all-start.1
  370.0 1.8 fusion.34
  371.7 4.0 collective-permute-start
  375.7 1.1 fusion.11
  376.8 1.2 collective-permute-done
  378.1 1.6 fusion.35
  379.7 0.5 fusion.10
  380.2 1.2 multiply_convert_fusion
  381.4 0.5 fusion.38
  381.9 1.3 collective-permute-start.2
  383.2 1.1 convolution_convert_fusion
  384.3 8.5 %all-to-all-start.5 = ((bf16[8,64,128]{2,1,0:T(8,128)(2,1)}), bf16[8,64,128]{2,1,0:T(8,128)(2,1)S(1)}, u32[]{:S(2)}, u32[]{:S(2)}) async-start(bf16[8,64,128]{2,1,0:T(8,128)(2,1)} %bitcast.17), calls=%async_computation.6 | async-start | bytes 262144 | tf_op jit(solution)/shard_map/all_to_all | solution.py:256
  392.8 0.7 fusion.12
  393.5 6.7 %all-to-all-done.5 = bf16[8,64,128]{2,1,0:T(8,128)(2,1)S(1)} async-done(((bf16[8,64,128]{2,1,0:T(8,128)(2,1)}), bf16[8,64,128]{2,1,0:T(8,128)(2,1)S(1)}, u32[]{:S(2)}, u32[]{:S(2)}) %all-to-all-start.5) | async-done | bytes 131104 | tf_op jit(solution)/shard_map/all_to_all | solution.py:256
  400.1 3.4 all-to-all-start.6
  403.6 2.0 all_gather.19
  405.6 4.7 convolution_bitcast_fusion
  410.3 0.5 all-to-all-done.6
  410.8 3.4 psum.37
  414.2 1.7 fusion
  415.9 0.1 copy.52
  416.0 31.4 %all_to_all.101 = bf16[128,8,512]{2,0,1:T(8,128)(2,1)S(1)} all-to-all(bf16[128,8,512]{2,0,1:T(8,128)(2,1)S(1)} %bitcast.78), channel_id=1, replica_groups=mesh['grp'=2,'seq'=8,'lat'=2] {'seq'}, dimensions={1} | all-to-all | bytes 2097152 | tf_op jit(solution)/shard_map/all_to_all | solution.py:276
  447.4 0.4 fusion.4
  447.8 31.4 %psum.38 = f32[1024]{0:T(1024)S(1)} all-reduce(f32[1024]{0:T(1024)S(1)} %fusion.4), channel_id=1, replica_groups=mesh['grp'=2,'seq'=8,'lat'=2] {'seq','lat'}, use_global_device_ids=true, to_apply=%region_12.13 | all-reduce | flops 1024 | bytes 8192 | tf_op jit(solution)/shard_map/psum | solution.py:279
  479.2 0.5 fusion.6
  479.7 16.2 %fusion.8 = f32[1024,1,32]{2,1,0:T(1,128)S(1)} fusion(bf16[1024,32,512]{2,1,0:T(8,128)(2,1)} %bitcast.72, bf16[1024,512,1]{1,0,2:T(8,128)(2,1)S(1)} %bitcast.82), kind=kOutput, calls=%fused_computation.20 | convolution fusion | flops 33554432 | bytes 34734080 | tf_op jit(solution)/shard_map/bc,bkc->bk/dot_general | solution.py:285
  496.0 0.9 copy.42
  496.9 59.0 %reduce-scatter.5.cloned.1.call-done = f32[128,32]{0,1:T(8,128)} async-done(((f32[1024,32]{0,1:T(8,128)}), f32[128,32]{0,1:T(8,128)}) %reduce-scatter.5.cloned.1.call-update) | async-done | bytes 16400 | tf_op jit(solution)/shard_map/reduce_scatter | solution.py:293
  555.9 4.6 psum.39
  (46 shorter events, 0.4 us)
Async XLA Ops:
  6.5 282.5 %copy-start = (s32[8,3]{0,1:T(4,128)S(1)}, s32[8,3]{0,1:T(4,128)}, u32[]{:S(2)}) copy-start(s32[8,3]{0,1:T(4,128)} %param.19) | copy-start | bytes 292
  6.5 2.3 copy-start.5
  6.5 35.6 %copy-start.7 = (bf16[128,32]{0,1:T(8,128)(2,1)S(1)}, bf16[128,32]{0,1:T(8,128)(2,1)}, u32[]{:S(2)}) copy-start(bf16[128,32]{0,1:T(8,128)(2,1)} %param.11) | copy-start | bytes 24580
  6.5 319.3 %all-gather.3.cloned.1.call-start = ((), (), s32[]{:S(2)}) async-start(), calls=%async_computation.10 | async-start | bytes 9437184 | tf_op jit(solution)/shard_map/all_gather | solution.py:216
  8.9 60.8 %copy-start.8 = (bf16[512]{0:T(512)(128)(2,1)S(1)}, bf16[512]{0:T(512)(128)(2,1)}, u32[]{:S(2)}) copy-start(bf16[512]{0:T(512)(128)(2,1)} %param.13) | copy-start | bytes 3076
  8.9 60.8 %copy-start.9 = (bf16[512]{0:T(512)(128)(2,1)S(1)}, bf16[512]{0:T(512)(128)(2,1)}, u32[]{:S(2)}) copy-start(bf16[512]{0:T(512)(128)(2,1)} %param.14) | copy-start | bytes 3076
  284.5 33.9 %copy-start.4 = (bf16[128,128]{1,0:T(8,128)(2,1)S(1)}, bf16[128,128]{1,0:T(8,128)(2,1)}, u32[]{:S(2)}) copy-start(bf16[128,128]{1,0:T(8,128)(2,1)} %param.18) | copy-start | bytes 98308
  284.5 33.9 %all-to-all-start = ((bf16[8,128,512]{2,1,0:T(8,128)(2,1)}), bf16[8,128,512]{2,1,0:T(8,128)(2,1)S(1)}, u32[]{:S(2)}, u32[]{:S(2)}) async-start(bf16[8,128,512]{2,1,0:T(8,128)(2,1)} %bitcast.4), calls=%async_computation | async-start | bytes 2097152 | tf_op jit(solution)/shard_map/all_to_all | solution.py:214
  288.2 60.5 %all-gather.5.cloned.1.call-start = ((), (), s32[]{:S(2)}) async-start(), calls=%async_computation.12 | async-start | bytes 1179648 | tf_op jit(solution)/shard_map/all_gather | solution.py:217
  319.1 18.0 %all-to-all-start.3 = ((bf16[8,64,128]{2,1,0:T(8,128)(2,1)}), bf16[8,64,128]{2,1,0:T(8,128)(2,1)S(1)}, u32[]{:S(2)}, u32[]{:S(2)}) async-start(bf16[8,64,128]{2,1,0:T(8,128)(2,1)} %bitcast.12), calls=%async_computation.4 | async-start | bytes 262144 | tf_op jit(solution)/shard_map/all_to_all | solution.py:237
  322.7 38.5 %reduce-scatter.3.cloned.1.call-start = ((), (), s32[]{:S(2)}) async-start(), calls=%async_computation.11 | async-start | bytes 786432 | tf_op jit(solution)/shard_map/reduce_scatter | solution.py:222
  337.1 17.4 %all-to-all-start.4 = ((bf16[8,64,128]{2,1,0:T(8,128)(2,1)}), bf16[8,64,128]{2,1,0:T(8,128)(2,1)S(1)}, u32[]{:S(2)}, u32[]{:S(2)}) async-start(bf16[8,64,128]{2,1,0:T(8,128)(2,1)} %bitcast.14), calls=%async_computation.5 | async-start | bytes 262144 | tf_op jit(solution)/shard_map/all_to_all | solution.py:233
  343.0 27.0 %collective-permute-start.1 = (bf16[512,128]{1,0:T(8,128)(2,1)S(1)}, bf16[512,128]{1,0:T(8,128)(2,1)}, u32[]{:S(2)}, u32[]{:S(2)}) collective-permute-start(bf16[512,128]{1,0:T(8,128)(2,1)S(1)} %bitcast.83), channel_id=1, source_target_pairs={{0,2},{2,4},{4,6},{6,8},{8,10},{10,12},{12,14},{1,3},{3,5},{5,7},{... | collective-permute-start | bytes 393224 | tf_op jit(solution)/shard_map/ppermute | solution.py:17
  348.7 10.4 %copy-start.2 = (s32[512,1024]{1,0:T(8,128)S(1)}, s32[512,1024]{1,0:T(8,128)}, u32[]{:S(2)}) copy-start(s32[512,1024]{1,0:T(8,128)} %select_reduce_fusion) | copy-start | bytes 6291460
  354.4 12.2 %copy-start.3 = (bf16[8,64,128]{2,1,0:T(8,128)(2,1)}, bf16[8,64,128]{2,1,0:T(8,128)(2,1)S(1)}, u32[]{:S(2)}) copy-start(bf16[8,64,128]{2,1,0:T(8,128)(2,1)S(1)} %all-to-all-done.4) | copy-start | bytes 393220
  355.1 11.4 %all-to-all-start.2 = ((bf16[8,64,128]{2,1,0:T(8,128)(2,1)}), bf16[8,64,128]{2,1,0:T(8,128)(2,1)S(1)}, u32[]{:S(2)}, u32[]{:S(2)}) async-start(bf16[8,64,128]{2,1,0:T(8,128)(2,1)} %bitcast.91), calls=%async_computation.3 | async-start | bytes 262144 | tf_op jit(solution)/shard_map/all_to_all | solution.py:234
  366.6 11.5 %all-to-all-start.1 = ((bf16[8,64,128]{2,1,0:T(8,128)(2,1)}), bf16[8,64,128]{2,1,0:T(8,128)(2,1)S(1)}, u32[]{:S(2)}, u32[]{:S(2)}) async-start(bf16[8,64,128]{2,1,0:T(8,128)(2,1)} %bitcast.8), calls=%async_computation.2 | async-start | bytes 262144 | tf_op jit(solution)/shard_map/all_to_all | solution.py:232
  371.7 6.3 %collective-permute-start = (bf16[512,128]{1,0:T(8,128)(2,1)S(1)}, bf16[512,128]{1,0:T(8,128)(2,1)S(1)}, u32[]{:S(2)}, u32[]{:S(2)}) collective-permute-start(bf16[512,128]{1,0:T(8,128)(2,1)S(1)} %bitcast.85), channel_id=1, source_target_pairs={{0,2},{2,4},{4,6},{6,8},{8,10},{10,12},{12,14},{1,3},{3,5},{5,7},{... | collective-permute-start | bytes 393224 | tf_op jit(solution)/shard_map/ppermute | solution.py:17
  378.1 2.1 copy-start.6
  381.9 10.9 %collective-permute-start.2 = (bf16[512,128]{1,0:T(8,128)(2,1)S(1)}, bf16[512,128]{1,0:T(8,128)(2,1)S(1)}, u32[]{:S(2)}, u32[]{:S(2)}) collective-permute-start(bf16[512,128]{1,0:T(8,128)(2,1)S(1)} %slice.15), channel_id=1, source_target_pairs={{2,0},{4,2},{6,4},{8,6},{10,8},{12,10},{14,12},{3,1},{5,3},{7,5},{... | collective-permute-start | bytes 393224 | tf_op jit(solution)/shard_map/ppermute | solution.py:17
  384.3 15.9 %all-to-all-start.5 = ((bf16[8,64,128]{2,1,0:T(8,128)(2,1)}), bf16[8,64,128]{2,1,0:T(8,128)(2,1)S(1)}, u32[]{:S(2)}, u32[]{:S(2)}) async-start(bf16[8,64,128]{2,1,0:T(8,128)(2,1)} %bitcast.17), calls=%async_computation.6 | async-start | bytes 262144 | tf_op jit(solution)/shard_map/all_to_all | solution.py:256
  400.1 10.7 %all-to-all-start.6 = ((bf16[8,64,128]{2,1,0:T(8,128)(2,1)}), bf16[8,64,128]{2,1,0:T(8,128)(2,1)S(1)}, u32[]{:S(2)}, u32[]{:S(2)}) async-start(bf16[8,64,128]{2,1,0:T(8,128)(2,1)} %bitcast.20), calls=%async_computation.7 | async-start | bytes 262144 | tf_op jit(solution)/shard_map/all_to_all | solution.py:259
  403.5 152.4 %reduce-scatter.5.cloned.1.call-start = ((), (), s32[]{:S(2)}) async-start(), calls=%async_computation.13 | async-start | bytes 147456 | tf_op jit(solution)/shard_map/reduce_scatter | solution.py:293
  479.7 80.7 %copy-start.1 = (s32[8,3]{0,1:T(4,128)S(1)}, s32[8,3]{0,1:T(4,128)}, u32[]{:S(2)}) copy-start(s32[8,3]{0,1:T(4,128)} %param.19) | copy-start | bytes 292
Sparse Core Ops, SparseCore 0:
  9.4 130.3 all-gather.2
  291.2 48.4 all-gather.4
  342.0 6.8 reduce-scatter.2
  497.0 58.8 reduce-scatter.4

commit v2 on v1

--- a/solution.py
+++ b/solution.py
@@ -1,3 +1,4 @@
+import functools
 import math
 
 import jax
@@ -167,7 +168,7 @@
     return (query_grad.astype(jnp.bfloat16), key_gradient[:range_len], key_gradient[range_len:])
 
 
-def local(
+def local_any(
     codes_idx,
     codes_val,
     decoder,
@@ -195,16 +196,8 @@
         lax.all_gather(codes_val, "seq", axis=0, tiled=True),
     )
     features = decoder_offset_bias.shape[0]
-    picked_rows = None
-    if features % LANES == 0:
-        picked_rows = gather_rows(decoder[0], all_idx).reshape(*all_idx.shape, features)
-        residual = jnp.einsum(
-            "bk,bkc->bc", every_code_value, picked_rows, preferred_element_type=jnp.float32
-        )
-        residual = residual + decoder_offset_bias.astype(jnp.float32)[None, :]
-    else:
-        dec_local = decoder.reshape(decoder.shape[1] * LATENTS_PER_ROW, features)
-        residual = decode_rows(dec_local, all_idx, every_code_value, decoder_offset_bias)
+    dec_local = decoder.reshape(decoder.shape[1] * LATENTS_PER_ROW, features)
+    residual = decode_rows(dec_local, all_idx, every_code_value, decoder_offset_bias)
     residual = residual.astype(jnp.bfloat16)
     resid_f32 = residual.astype(jnp.float32)
     squares = lax.psum(jnp.sum(resid_f32 * resid_f32, axis=1), ("seq", "lat"))
@@ -281,17 +274,244 @@
         gain_f32[None, :] * inv_rms[:, None] * grad_cols
         - resid_f32 * (inv_rms * inv_rms * inv_rms * inner_sum / model_width)[:, None]
     )
-    if picked_rows is not None:
-        grad_part = jnp.einsum(
-            "bc,bkc->bk",
-            resid_grad.astype(jnp.bfloat16),
-            picked_rows,
-            preferred_element_type=jnp.float32,
-        )
-    else:
-        grad_part = code_grads(dec_local, all_idx, resid_grad)
+    grad_part = code_grads(dec_local, all_idx, resid_grad)
     grad_seq = lax.psum_scatter(grad_part, "seq", scatter_dimension=0, tiled=True)
     return lax.psum(grad_seq, "lat")
+
+
+def exchange_kernel(axes, lanes_of, count, kinds, *refs):
+    sources, results = refs[:count], refs[count : 2 * count]
+    send_sem, recv_sem, local_sem = refs[2 * count :]
+    peers = math.prod(lanes_of)
+    me = lax.axis_index(axes[0])
+    if len(axes) > 1:
+        me = me * lanes_of[1] + lax.axis_index(axes[1])
+
+    def device(peer):
+        if len(axes) > 1:
+            return {axes[0]: peer // lanes_of[1], axes[1]: lax.rem(peer, lanes_of[1])}
+        return {axes[0]: peer}
+
+    def source(a, peer):
+        if kinds[a] == "gather":
+            return sources[a]
+        return sources[a].at[peer // (peers // sources[a].shape[0])]
+
+    barrier = pltpu.get_barrier_semaphore()
+    for d in range(1, peers):
+        pl.semaphore_signal(
+            barrier,
+            inc=1,
+            device_id=device(lax.rem(me + d, peers)),
+            device_id_type=pl.DeviceIdType.MESH,
+        )
+    own = [
+        pltpu.make_async_copy(source(a, me), results[a].at[me], local_sem.at[a])
+        for a in range(count)
+    ]
+    for copy in own:
+        copy.start()
+    pl.semaphore_wait(barrier, peers - 1)
+
+    def remote(a, d, slot):
+        peer = lax.rem(me + d, peers)
+        return pltpu.make_async_remote_copy(
+            src_ref=source(a, peer),
+            dst_ref=results[a].at[slot],
+            send_sem=send_sem.at[a, d],
+            recv_sem=recv_sem.at[a, d],
+            device_id=device(peer),
+            device_id_type=pl.DeviceIdType.MESH,
+        )
+
+    for a in range(count):
+        for d in range(1, peers):
+            remote(a, d, me).start()
+    for copy in own:
+        copy.wait()
+    for a in range(count):
+        for d in range(1, peers):
+            remote(a, d, lax.rem(me + peers - d, peers)).wait_recv()
+    for a in range(count):
+        for d in range(1, peers):
+            remote(a, d, me).wait_send()
+
+
+def exchange(axes, collective_id, *items):
+    kinds = [kind for kind, _ in items]
+    arrays = [array for _, array in items]
+    sizes = [lax.axis_size(axis) for axis in axes]
+    peers = math.prod(sizes)
+    shapes = [
+        jax.ShapeDtypeStruct((peers,) + (a.shape if kind == "gather" else a.shape[1:]), a.dtype)
+        for kind, a in items
+    ]
+    count = len(items)
+    return pl.pallas_call(
+        functools.partial(exchange_kernel, axes, sizes, count, kinds),
+        out_shape=shapes,
+        in_specs=[pl.BlockSpec(memory_space=pltpu.VMEM)] * count,
+        out_specs=[pl.BlockSpec(memory_space=pltpu.VMEM)] * count,
+        scratch_shapes=[
+            pltpu.SemaphoreType.DMA((count, peers)),
+            pltpu.SemaphoreType.DMA((count, peers)),
+            pltpu.SemaphoreType.DMA((count,)),
+        ],
+        compiler_params=pltpu.CompilerParams(
+            collective_id=collective_id,
+            has_side_effects=True,
+            vmem_limit_bytes=32 * 1024 * 1024,
+        ),
+    )(*arrays)
+
+
+def as_tile(vectors):
+    missing = LANES - vectors.shape[-1]
+    padded = jnp.pad(vectors, [(0, 0)] * (vectors.ndim - 1) + [(0, missing)])
+    return jnp.broadcast_to(padded[..., None, :], padded.shape[:-1] + (8, LANES))
+
+
+def local(
+    codes_idx,
+    codes_val,
+    decoder,
+    decoder_offset_bias,
+    norm_gain,
+    w_query,
+    w_key,
+    orig_queries,
+    orig_keys,
+    mask_layout,
+):
+    seq_count, lat_count = lax.axis_size("seq"), lax.axis_size("lat")
+    features = decoder_offset_bias.shape[0]
+    heads_here = orig_queries.shape[0]
+    tok_rows, top_count = codes_idx.shape
+    ranges = seq_count // heads_here
+    if features % LANES or ranges != lat_count:
+        return local_any(
+            codes_idx,
+            codes_val,
+            decoder,
+            decoder_offset_bias,
+            norm_gain,
+            w_query,
+            w_key,
+            orig_queries,
+            orig_keys,
+            mask_layout,
+        )
+    peers = seq_count * lat_count
+    head_dim = orig_keys.shape[1]
+    all_heads = heads_here * lat_count
+    model_width = features * peers
+    tokens = tok_rows * seq_count
+    range_len = tokens // ranges
+    sub = tok_rows // ranges
+    block_len = tokens // mask_layout.shape[0]
+    this_range = lax.axis_index("seq") % ranges
+    both = ("seq", "lat")
+
+    def by_position(array):
+        cut = array.reshape(seq_count, ranges, sub, *array.shape[1:])
+        return jnp.swapaxes(cut, 0, 1).reshape(array.shape)
+
+    def by_token(array):
+        cut = array.reshape(ranges, seq_count, sub, *array.shape[1:])
+        return jnp.swapaxes(cut, 0, 1).reshape(array.shape)
+
+    idx_all, val_all, query_old, keys_old = exchange(
+        ("seq",),
+        0,
+        ("gather", codes_idx),
+        ("gather", codes_val),
+        ("scatter", orig_queries.reshape(seq_count, sub, head_dim)),
+        ("gather", orig_keys),
+    )
+    idx_all = by_position(idx_all.reshape(tokens, top_count))
+    val_all = by_position(val_all.reshape(tokens, top_count))
+    query_old = query_old.reshape(range_len, head_dim)
+    keys_old = by_position(keys_old.reshape(tokens, head_dim))
+
+    picked_rows = gather_rows(decoder[0], idx_all).reshape(tokens, top_count, features)
+    residual = jnp.einsum("bk,bkc->bc", val_all, picked_rows, preferred_element_type=jnp.float32)
+    residual = (residual + decoder_offset_bias.astype(jnp.float32)[None, :]).astype(jnp.bfloat16)
+    resid_f32 = residual.astype(jnp.float32)
+    gain_f32 = norm_gain.astype(jnp.float32)
+    squares = jnp.sum(resid_f32 * resid_f32, axis=1)
+    scaled = (resid_f32 * gain_f32[None, :]).astype(jnp.bfloat16)
+
+    query_part = jnp.dot(scaled, w_query, preferred_element_type=jnp.float32).astype(jnp.bfloat16)
+    query_part = query_part.reshape(ranges, range_len, lat_count, heads_here, head_dim)
+    query_part = jnp.transpose(query_part, (3, 0, 2, 1, 4)).reshape(peers, range_len, head_dim)
+    key_part = jnp.dot(scaled, w_key, preferred_element_type=jnp.float32).astype(jnp.bfloat16)
+    query_parts, key_parts, square_parts = exchange(
+        both,
+        1,
+        ("scatter", query_part),
+        ("scatter", by_token(key_part).reshape(peers, sub, head_dim)),
+        ("scatter", as_tile(by_token(squares).reshape(peers, sub))),
+    )
+    query_raw = jnp.sum(query_parts.astype(jnp.float32), axis=0)
+    key_raw = jnp.sum(key_parts.astype(jnp.float32), axis=0)
+    inv_here = lax.rsqrt(jnp.sum(square_parts[:, 0, :sub], axis=0) / model_width + EPSILON)
+    key_here = (key_raw * inv_here[:, None]).astype(jnp.bfloat16)
+    keys_new, inv_tiles = exchange(both, 2, ("gather", key_here), ("gather", as_tile(inv_here)))
+    keys_new = by_position(keys_new.reshape(tokens, head_dim))
+    inv_rms = by_position(inv_tiles[:, 0, :sub].reshape(tokens))
+    first_pos = this_range * range_len
+    inv_range = lax.dynamic_slice_in_dim(inv_rms, first_pos, range_len, 0)
+    query_new = (query_raw * inv_range[:, None]).astype(jnp.bfloat16)
+
+    def window(keys):
+        padded = jnp.pad(keys, ((range_len, 0), (0, 0)))
+        return lax.dynamic_slice_in_dim(padded, first_pos, 2 * range_len, 0)
+
+    query_grad, key_grad_prev, key_grad_own = attend(
+        query_new,
+        query_old,
+        window(keys_new),
+        window(keys_old),
+        mask_layout,
+        first_pos,
+        block_len,
+    )
+    key_grad = lax.dynamic_update_slice_in_dim(
+        jnp.zeros(((ranges + 1) * range_len, head_dim), jnp.float32),
+        jnp.concatenate([key_grad_prev, key_grad_own], axis=0),
+        first_pos,
+        0,
+    )[range_len:]
+    query_inner = jnp.sum(query_grad.astype(jnp.float32) * query_new.astype(jnp.float32), axis=1)
+    query_grads, key_grad_parts, inner_parts = exchange(
+        both,
+        3,
+        ("gather", query_grad),
+        ("scatter", by_token(key_grad.astype(jnp.bfloat16)).reshape(peers, sub, head_dim)),
+        ("gather", query_inner.reshape(range_len // LANES, LANES)),
+    )
+    key_grad_here = jnp.sum(key_grad_parts.astype(jnp.float32), axis=0).astype(jnp.bfloat16)
+    (key_grads,) = exchange(both, 4, ("gather", key_grad_here))
+    key_grads = by_position(key_grads.reshape(tokens, head_dim))
+
+    inner = jnp.sum(
+        inner_parts.reshape(heads_here, ranges, lat_count, range_len), axis=(0, 2)
+    ).reshape(tokens)
+    inner = inner + jnp.sum(key_grads.astype(jnp.float32) * keys_new.astype(jnp.float32), axis=1)
+    query_grads = query_grads.reshape(heads_here, ranges, lat_count, range_len, head_dim)
+    query_grads = jnp.transpose(query_grads, (1, 3, 2, 0, 4)).reshape(tokens, all_heads * head_dim)
+    normed_grad = jnp.einsum("te,de->td", query_grads, w_query, preferred_element_type=jnp.float32)
+    normed_grad = normed_grad + jnp.einsum(
+        "te,de->td", key_grads, w_key, preferred_element_type=jnp.float32
+    )
+    resid_grad = (
+        gain_f32[None, :] * inv_rms[:, None] * normed_grad
+        - resid_f32 * (inv_rms * inv_rms * inner / model_width)[:, None]
+    ).astype(jnp.bfloat16)
+    grad_part = jnp.einsum("bc,bkc->bk", resid_grad, picked_rows, preferred_element_type=jnp.float32)
+    grad_part = by_token(grad_part).reshape(seq_count, tok_rows * top_count // LANES, LANES)
+    (grad_parts,) = exchange(both, 5, ("scatter", grad_part))
+    return jnp.sum(grad_parts, axis=0).reshape(tok_rows, top_count)
 
 
 def solution(mesh):

time: 569 us -> 417 us (0.73)
  Pallas kernels: 171 us -> 351 us
  blocking collectives: 166 us -> 0 us
  waiting for transfers between devices: 99 us -> 0 us
  starting transfers between devices: 42.5 us -> 0 us
  matrix products: 49.2 us -> 36 us
  between operations: 13.5 us -> 0.54 us
  local copies, waits for them, and re-layouts: 9.77 us -> 21.1 us
  other arithmetic: 16 us -> 8.01 us
    pallas_call x0 -> x6, Pallas kernels: none -> 180 us  [exchange(): pl.pallas_call(functools.partial(exchange_kernel, axes, sizes, count, kin...]
    psum x5 -> x0, blocking collectives: 72.5 us -> none  [the longest x1 31.4 us: local(): lax.psum(jnp.sum(grad_cols * gain_f32[None, :] * resid_f32, axis=1), ('se...]
    all_gather x3 -> x0, blocking collectives: 62 us -> none  [the longest x1 32.9 us: local(): lax.all_gather(codes_idx, 'seq', axis=0, tiled=True)]
    reduce_scatter x2 -> x0, waiting for transfers between devices: 59 us -> none  [the longest x1 59 us: local(): lax.psum_scatter(grad_part, 'seq', scatter_dimension=0, tiled=True)]
    all_to_all x7 -> x0, waiting for transfers between devices: 38 us -> none  [the longest x1 27 us: local(): lax.all_to_all(normed, 'seq', split_axis=0, concat_axis=1, tiled=True)]
    all_to_all x7 -> x0, starting transfers between devices: 32.5 us -> none  [the longest x1 8.54 us: local(): lax.all_to_all(query_grad_wide.astype(jnp.bfloat16), 'seq', split_axis=0,...]
    all_to_all x1 -> x0, blocking collectives: 31.4 us -> none  [local(): lax.all_to_all(normed_grad, 'seq', split_axis=1, concat_axis=0, tiled=True)]
    reshape x1 -> x12, local copies, waits for them, and re-layouts: 0.17 us -> 13.2 us  [the longest x2 4.8 us: local(): query_part.reshape(ranges, range_len, lat_count, heads_here, head_dim)]
  transfers between devices with their start and end apart: 14 -> 0, of which waited for: 6 -> 0; matrix products, arithmetic and copies ran while one was open for 9% -> 0% of each run, Pallas kernels for 30% -> 0%
where the time goes in v2:
time: 417 us; the launch traced here: 416 us
  Pallas kernels  351 us (84%)
  matrix products  36 us (9%)
  local copies, waits for them, and re-layouts  21.1 us (5%)
  other arithmetic  8.01 us (2%)
    pallas_call x6, Pallas kernels, exchange(): pl.pallas_call(functools.partial(exchange_kernel, axes, sizes, count, kin...  180 us
    pallas_call x1, Pallas kernels, gather_rows(): pl.pallas_call(gather_kernel, out_shape=jax.ShapeDtypeStruct((pairs, feat...  171 us
    dot_general x1, matrix products, local(): jnp.einsum('bc,bkc->bk', resid_grad, picked_rows, preferred_element_type=...  16.5 us
    dot_general x1, matrix products, local(): jnp.einsum('bk,bkc->bc', val_all, picked_rows, preferred_element_type=jnp...  13 us

profile of v2, /device:TPU:0, one launch (start us, length us, event | category | flops | bytes accessed | tf_op | source)
XLA Modules:
  0.0 416.2 jit_solution(7571054271588868459)
XLA Ops:
  0.0 0.9 copy.50.refs_0_
  0.9 0.8 copy.51.refs_1_
  1.7 0.9 copy-done.5
  2.6 0.8 copy-done.6
  3.4 30.9 %shard_map.100 = (s32[8,128,32]{2,1,0:T(8,128)S(1)}, bf16[8,128,32]{2,1,0:T(8,128)(2,1)S(1)}, bf16[8,64,128]{2,1,0:T(8,128)(2,1)S(1)}, bf16[8,128,128]{2,1,0:T(8,128)(2,1)S(1)}) custom-call(s32[128,32]{1,0:T(8,128)S(1)} %copy.50.refs_0_, bf16[128,32]{1,0:T(8,128)(2,1)S(1)} %copy.51.refs_1_, bf16[8,64,128]{2,1,0:T(8,128)(2,1)S(1)} %bitcast.100, ...), custom_call_target="tpu_custom_call" | custom-call | tf_op jit(solution)/shard_map/pallas_call | solution.py:350
  34.4 0.6 copy-done.3
  35.0 0.2 reshape_reshape.32
  35.2 0.1 fusion.13.idx_ref
  35.3 170.9 %shard_map.101 = bf16[32768,512]{1,0:T(8,128)(2,1)} custom-call(s32[32768]{0:T(1024)S(1)} %fusion.13.idx_ref, bf16[16384,2048]{1,0:T(8,128)(2,1)} %bitcast.5.block_ref), custom_call_target="tpu_custom_call" | custom-call | tf_op jit(solution)/shard_map/pallas_call | solution.py:74
  206.2 0.2 copy.52
  206.4 0.1 reshape.185
  206.5 1.1 copy.66
  207.6 13.0 %fusion.33 = f32[1024,1,512]{2,1,0:T(1,128)S(1)} fusion(bf16[1024,32,1]{1,2,0:T(2,128)(2,1)} %copy.66, bf16[1024,32,512]{2,1,0:T(8,128)(2,1)} %bitcast.102), kind=kOutput, calls=%fused_computation.84 | convolution fusion | flops 33554432 | bytes 35717120 | tf_op jit(solution)/shard_map/bk,bkc->bc/dot_general | solution.py:437
  220.6 0.0 copy-start.14
  220.7 0.3 fusion.1
  221.0 0.3 copy-done.14
  221.3 0.6 copy-done.7
  222.0 1.3 convolution_convert_fusion
  223.2 2.7 reshape.169
  225.9 2.1 copy.54
  228.0 0.0 copy-done.8
  228.0 0.0 copy-done.10
  228.1 0.4 convolution_convert_fusion.1
  228.5 0.1 reshape.172
  228.6 59.6 %shard_map.102 = (bf16[16,512,128]{2,1,0:T(8,128)(2,1)S(1)}, bf16[16,64,128]{2,1,0:T(8,128)(2,1)S(1)}, f32[16,8,128]{2,1,0:T(8,128)S(1)}) custom-call(bf16[16,512,128]{2,1,0:T(8,128)(2,1)S(1)} %bitcast.88, bf16[16,64,128]{2,1,0:T(8,128)(2,1)S(1)} %bitcast.92, f32[16,8,128]{2,1,0:T(8,128)S(1)} %broadcast_in_dim.26.refs_2_), custom_call_target="tpu_custom_call" | custom-call | tf_op jit(solution)/shard_map/pallas_call | solution.py:350
  288.2 1.3 copy-done.1
  289.6 0.1 multiply_convert_fusion.2.refs_0_
  289.7 12.7 %shard_map.103 = (bf16[16,64,128]{2,1,0:T(8,128)(2,1)S(1)}, f32[16,8,128]{2,1,0:T(8,128)S(1)}) custom-call(bf16[64,128]{1,0:T(8,128)(2,1)S(1)} %multiply_convert_fusion.2.refs_0_, f32[8,128]{1,0:T(8,128)S(1)} %broadcast_in_dim.27.refs_1_), custom_call_target="tpu_custom_call" | custom-call | tf_op jit(solution)/shard_map/pallas_call | solution.py:350
  302.4 0.0 copy-start.2
  302.5 0.1 mul.100
  302.5 0.1 dynamic_slice.13
  302.6 1.9 convert_reduce_fusion
  304.5 0.1 multiply_convert_fusion.1
  304.7 0.1 constant_dynamic-slice_fusion
  304.8 0.1 broadcast_bitcast_fusion
  304.9 0.2 subtract_add_fusion
  305.1 1.1 select_reduce_fusion
  306.2 0.6 compare_and_fusion
  306.8 0.0 copy-done.2
  306.9 0.0 copy-start.4
  306.9 0.8 fusion.32
  307.7 0.5 fusion.7
  308.2 0.8 fusion.31
  309.0 0.5 fusion.8
  309.5 1.1 multiply_convert_fusion
  310.7 0.6 convolution_dynamic-update-slice_fusion
  311.4 0.6 multiply_reduce_fusion.1
  312.0 57.4 %shard_map.104 = (bf16[16,512,128]{2,1,0:T(8,128)(2,1)S(1)}, bf16[16,64,128]{2,1,0:T(8,128)(2,1)S(1)}, f32[16,4,128]{2,1,0:T(4,128)S(1)}) custom-call(bf16[512,128]{1,0:T(8,128)(2,1)S(1)} %get-tuple-element.36.refs_0_, bf16[16,64,128]{2,1,0:T(8,128)(2,1)S(1)} %bitcast.95, f32[4,128]{1,0:T(4,128)S(1)} %bitcast.101), custom_call_target="tpu_custom_call" | custom-call | tf_op jit(solution)/shard_map/pallas_call | solution.py:350
  369.4 8.3 %shard_map.105 = bf16[16,64,128]{2,1,0:T(8,128)(2,1)S(1)} custom-call(bf16[64,128]{1,0:T(8,128)(2,1)S(1)} %reduce_sum.121.refs_0_), custom_call_target="tpu_custom_call" | custom-call | tf_op jit(solution)/shard_map/pallas_call | solution.py:350
  377.7 1.2 multiply_reduce_fusion
  378.9 0.1 reduce_sum.124
  379.0 2.9 copy.83
  382.0 3.2 reshape.179
  385.2 0.0 copy-start.11
  385.2 1.3 fusion.34
  386.6 0.7 fusion.9
  387.2 16.5 %fusion.5 = f32[1024,1,32]{2,1,0:T(1,128)S(1)} fusion(bf16[1024,32,512]{2,1,0:T(8,128)(2,1)} %bitcast.103, bf16[1024,512,1]{1,0,2:T(8,128)(2,1)S(1)} %fusion.9), kind=kOutput, calls=%fused_computation.12 | convolution fusion | flops 33554432 | bytes 34734080 | tf_op jit(solution)/shard_map/bc,bkc->bk/dot_general | solution.py:511
  403.7 0.3 copy.70
  404.0 0.1 reshape.183
  404.1 0.2 copy.64
  404.3 0.2 reshape_reshape.39.refs_0_
  404.5 10.9 %shard_map.106 = f32[16,32,128]{2,1,0:T(8,128)S(1)} custom-call(f32[8,32,128]{2,1,0:T(8,128)S(1)} %reshape_reshape.39.refs_0_), custom_call_target="tpu_custom_call" | custom-call | tf_op jit(solution)/shard_map/pallas_call | solution.py:350
  415.5 0.1 reshape.184
  415.5 0.7 copy.65
  (47 shorter events, 0.5 us)
Async XLA Ops:
  0.0 222.0 %copy-start = (bf16[512,1024]{1,0:T(8,128)(2,1)S(1)}, bf16[512,1024]{1,0:T(8,128)(2,1)}, u32[]{:S(2)}) copy-start(bf16[512,1024]{1,0:T(8,128)(2,1)} %param.15) | copy-start | bytes 3145732
  1.7 0.9 copy-start.5
  2.6 0.8 copy-start.6
  34.3 0.7 copy-start.3
  207.6 13.1 %copy-start.13 = (bf16[512]{0:T(512)(128)(2,1)S(1)}, bf16[512]{0:T(512)(128)(2,1)}, u32[]{:S(2)}) copy-start(bf16[512]{0:T(512)(128)(2,1)} %param.13) | copy-start | bytes 3076
  220.6 0.7 copy-start.14
  221.0 1.0 copy-start.7
  225.9 2.1 copy-start.8
  225.9 2.1 copy-start.10
  288.2 1.3 copy-start.1
  289.5 15.1 %copy-start.12 = (s32[8,3]{0,1:T(4,128)S(1)}, s32[8,3]{0,1:T(4,128)}, u32[]{:S(2)}) copy-start(s32[8,3]{0,1:T(4,128)} %param.19) | copy-start | bytes 292
  302.4 4.4 %copy-start.2 = (bf16[16,64,128]{2,1,0:T(8,128)(2,1)}, bf16[16,64,128]{2,1,0:T(8,128)(2,1)S(1)}, u32[]{:S(2)}) copy-start(bf16[16,64,128]{2,1,0:T(8,128)(2,1)S(1)} %get-tuple-element.23) | copy-start | bytes 786436
  306.9 1.3 copy-start.4
  385.2 1.3 copy-start.9
  385.2 1.3 copy-start.11

commit v3 on v2

--- a/solution.py
+++ b/solution.py
@@ -412,7 +412,7 @@
     this_range = lax.axis_index("seq") % ranges
     both = ("seq", "lat")
 
-    def by_position(array):
+    def by_position(array, sub=sub):
         cut = array.reshape(seq_count, ranges, sub, *array.shape[1:])
         return jnp.swapaxes(cut, 0, 1).reshape(array.shape)
 
@@ -420,18 +420,20 @@
         cut = array.reshape(ranges, seq_count, sub, *array.shape[1:])
         return jnp.swapaxes(cut, 0, 1).reshape(array.shape)
 
-    idx_all, val_all, query_old, keys_old = exchange(
+    flat_rows = tok_rows * top_count // LANES
+    old_half = lax.dynamic_slice_in_dim(orig_keys, lax.axis_index("lat") * sub, sub, 0)
+    idx_all, val_all, query_old, old_half = exchange(
         ("seq",),
         0,
-        ("gather", codes_idx),
-        ("gather", codes_val),
+        ("gather", codes_idx.reshape(flat_rows, LANES)),
+        ("gather", codes_val.reshape(flat_rows, LANES)),
         ("scatter", orig_queries.reshape(seq_count, sub, head_dim)),
-        ("gather", orig_keys),
-    )
-    idx_all = by_position(idx_all.reshape(tokens, top_count))
-    val_all = by_position(val_all.reshape(tokens, top_count))
+        ("gather", old_half),
+    )
+    idx_all = by_position(idx_all.reshape(seq_count * flat_rows, LANES), flat_rows // ranges)
+    val_all = by_position(val_all.reshape(seq_count * flat_rows, LANES), flat_rows // ranges)
+    val_all = val_all.reshape(tokens, top_count)
     query_old = query_old.reshape(range_len, head_dim)
-    keys_old = by_position(keys_old.reshape(tokens, head_dim))
 
     picked_rows = gather_rows(decoder[0], idx_all).reshape(tokens, top_count, features)
     residual = jnp.einsum("bk,bkc->bc", val_all, picked_rows, preferred_element_type=jnp.float32)
@@ -441,16 +443,28 @@
     squares = jnp.sum(resid_f32 * resid_f32, axis=1)
     scaled = (resid_f32 * gain_f32[None, :]).astype(jnp.bfloat16)
 
-    query_part = jnp.dot(scaled, w_query, preferred_element_type=jnp.float32).astype(jnp.bfloat16)
-    query_part = query_part.reshape(ranges, range_len, lat_count, heads_here, head_dim)
-    query_part = jnp.transpose(query_part, (3, 0, 2, 1, 4)).reshape(peers, range_len, head_dim)
-    key_part = jnp.dot(scaled, w_key, preferred_element_type=jnp.float32).astype(jnp.bfloat16)
+    wq_heads = w_query.reshape(features, all_heads, head_dim)
+    query_part = jnp.einsum("td,dhe->hte", scaled, wq_heads, preferred_element_type=jnp.float32)
+    key_part = jnp.dot(scaled, w_key, preferred_element_type=jnp.float32)
+    query_pair, key_pair, square_pair, keys_old = exchange(
+        ("lat",),
+        1,
+        ("scatter", query_part.astype(jnp.bfloat16).reshape(lat_count, -1, head_dim)),
+        ("scatter", key_part.astype(jnp.bfloat16).reshape(lat_count, range_len, head_dim)),
+        ("scatter", as_tile(squares.reshape(lat_count * seq_count, sub)).reshape(lat_count, -1, LANES)),
+        ("gather", old_half.reshape(range_len, head_dim)),
+    )
+    keys_old = keys_old.reshape(tokens, head_dim)
+
+    def pair_sum(array):
+        return jnp.sum(array.astype(jnp.float32), axis=0).astype(array.dtype)
+
     query_parts, key_parts, square_parts = exchange(
-        both,
-        1,
-        ("scatter", query_part),
-        ("scatter", by_token(key_part).reshape(peers, sub, head_dim)),
-        ("scatter", as_tile(by_token(squares).reshape(peers, sub))),
+        ("seq",),
+        6,
+        ("scatter", pair_sum(query_pair).reshape(seq_count, range_len, head_dim)),
+        ("scatter", pair_sum(key_pair).reshape(seq_count, sub, head_dim)),
+        ("scatter", pair_sum(square_pair).reshape(seq_count, 8, LANES)),
     )
     query_raw = jnp.sum(query_parts.astype(jnp.float32), axis=0)
     key_raw = jnp.sum(key_parts.astype(jnp.float32), axis=0)
@@ -484,23 +498,27 @@
     )[range_len:]
     query_inner = jnp.sum(query_grad.astype(jnp.float32) * query_new.astype(jnp.float32), axis=1)
     query_grads, key_grad_parts, inner_parts = exchange(
-        both,
+        ("seq",),
         3,
         ("gather", query_grad),
-        ("scatter", by_token(key_grad.astype(jnp.bfloat16)).reshape(peers, sub, head_dim)),
+        ("scatter", by_token(key_grad.astype(jnp.bfloat16)).reshape(seq_count, tok_rows, head_dim)),
         ("gather", query_inner.reshape(range_len // LANES, LANES)),
     )
-    key_grad_here = jnp.sum(key_grad_parts.astype(jnp.float32), axis=0).astype(jnp.bfloat16)
+    query_grads, key_grad_pair, inner_parts = exchange(
+        ("lat",),
+        7,
+        ("gather", query_grads.reshape(-1, head_dim)),
+        ("scatter", pair_sum(key_grad_parts).reshape(lat_count, sub, head_dim)),
+        ("gather", inner_parts.reshape(-1, LANES)),
+    )
+    key_grad_here = pair_sum(key_grad_pair)
     (key_grads,) = exchange(both, 4, ("gather", key_grad_here))
     key_grads = by_position(key_grads.reshape(tokens, head_dim))
 
-    inner = jnp.sum(
-        inner_parts.reshape(heads_here, ranges, lat_count, range_len), axis=(0, 2)
-    ).reshape(tokens)
+    inner = jnp.sum(inner_parts.reshape(all_heads, tokens), axis=0)
     inner = inner + jnp.sum(key_grads.astype(jnp.float32) * keys_new.astype(jnp.float32), axis=1)
-    query_grads = query_grads.reshape(heads_here, ranges, lat_count, range_len, head_dim)
-    query_grads = jnp.transpose(query_grads, (1, 3, 2, 0, 4)).reshape(tokens, all_heads * head_dim)
-    normed_grad = jnp.einsum("te,de->td", query_grads, w_query, preferred_element_type=jnp.float32)
+    query_grads = query_grads.reshape(all_heads, tokens, head_dim)
+    normed_grad = jnp.einsum("hte,dhe->td", query_grads, wq_heads, preferred_element_type=jnp.float32)
     normed_grad = normed_grad + jnp.einsum(
         "te,de->td", key_grads, w_key, preferred_element_type=jnp.float32
     )
@@ -509,8 +527,9 @@
         - resid_f32 * (inv_rms * inv_rms * inner / model_width)[:, None]
     ).astype(jnp.bfloat16)
     grad_part = jnp.einsum("bc,bkc->bk", resid_grad, picked_rows, preferred_element_type=jnp.float32)
-    grad_part = by_token(grad_part).reshape(seq_count, tok_rows * top_count // LANES, LANES)
+    grad_part = by_token(grad_part.astype(jnp.bfloat16)).reshape(seq_count, flat_rows, LANES)
     (grad_parts,) = exchange(both, 5, ("scatter", grad_part))
+    grad_parts = grad_parts.astype(jnp.float32)
     return jnp.sum(grad_parts, axis=0).reshape(tok_rows, top_count)
 
 

time: 417 us -> 350 us (0.84)
  Pallas kernels: 351 us -> 289 us
  local copies, waits for them, and re-layouts: 21.1 us -> 14 us
    pallas_call x6 -> x8, Pallas kernels: 180 us -> 119 us  [exchange(): pl.pallas_call(functools.partial(exchange_kernel, axes, sizes, count, kin...]
    reshape x7 -> x4, local copies, waits for them, and re-layouts: 12.2 us -> 0.85 us  [the longest x1 0.61 us: local(): inner = jnp.sum(inner_parts.reshape(all_heads, tokens), axis=0)]
    unnamed x35 -> x42, local copies, waits for them, and re-layouts: 6.43 us -> 9.33 us
where the time goes in v3:
time: 350 us; the launch traced here: 349 us
  Pallas kernels  289 us (83%)
  matrix products  36.3 us (10%)
  local copies, waits for them, and re-layouts  14 us (4%)
  other arithmetic  8.94 us (3%)
    pallas_call x1, Pallas kernels, gather_rows(): pl.pallas_call(gather_kernel, out_shape=jax.ShapeDtypeStruct((pairs, feat...  171 us
    pallas_call x8, Pallas kernels, exchange(): pl.pallas_call(functools.partial(exchange_kernel, axes, sizes, count, kin...  119 us
    dot_general x1, matrix products, local(): jnp.einsum('bc,bkc->bk', resid_grad, picked_rows, preferred_element_type=...  14.7 us
    dot_general x1, matrix products, local(): jnp.einsum('bk,bkc->bc', val_all, picked_rows, preferred_element_type=jnp...  13 us
    unnamed x42, local copies, waits for them, and re-layouts  9.33 us

profile of v3, /device:TPU:0, one launch (start us, length us, event | category | flops | bytes accessed | tf_op | source)
XLA Modules:
  0.0 349.3 jit_solution(5312260823745991018)
XLA Ops:
  0.0 0.8 constant_dynamic-slice_fusion.1.refs_3_
  0.8 0.8 copy.29
  1.6 0.1 reshape.185.refs_0_
  1.7 0.8 copy.30
  2.5 0.1 reshape.186.refs_1_
  2.6 0.9 copy-done.8
  3.5 16.7 %shard_map.100 = (s32[8,32,128]{2,1,0:T(8,128)S(1)}, bf16[8,32,128]{2,1,0:T(8,128)(2,1)S(1)}, bf16[8,64,128]{2,1,0:T(8,128)(2,1)S(1)}, bf16[8,64,128]{2,1,0:T(8,128)(2,1)S(1)}) custom-call(s32[32,128]{1,0:T(8,128)S(1)} %reshape.185.refs_0_, bf16[32,128]{1,0:T(8,128)(2,1)S(1)} %reshape.186.refs_1_, bf16[8,64,128]{2,1,0:T(8,128)(2,1)S(1)} %bitcast.120, ...), custom_call_target="tpu_custom_call" | custom-call | tf_op jit(solution)/shard_map/pallas_call | solution.py:350
  20.3 0.6 copy-done.6
  20.9 0.1 fusion.19.idx_ref
  21.0 170.9 %shard_map.101 = bf16[32768,512]{1,0:T(8,128)(2,1)} custom-call(s32[32768]{0:T(1024)S(1)} %fusion.19.idx_ref, bf16[16384,2048]{1,0:T(8,128)(2,1)} %bitcast.7.block_ref), custom_call_target="tpu_custom_call" | custom-call | tf_op jit(solution)/shard_map/pallas_call | solution.py:74
  191.9 1.0 reshape.218
  192.9 13.0 %fusion.39 = f32[1024,1,512]{2,1,0:T(1,128)S(1)} fusion(bf16[1024,32,1]{1,2,0:T(2,128)(2,1)} %reshape.218, bf16[1024,32,512]{2,1,0:T(8,128)(2,1)} %bitcast.126), kind=kOutput, calls=%fused_computation.93 | convolution fusion | flops 33554432 | bytes 35717120 | tf_op jit(solution)/shard_map/bk,bkc->bc/dot_general | solution.py:439
  206.0 0.3 fusion.1
  206.3 0.3 copy-done.18
  206.7 1.3 convolution_convert_fusion
  207.9 0.4 convolution_convert_fusion.1
  208.4 0.1 reshape.192
  208.5 0.9 copy-done.7
  209.4 3.3 shard_map.102
  212.7 1.3 copy-done.1
  214.0 0.7 copy-done.2
  214.7 0.7 copy-done.4
  215.4 0.6 copy-done.9
  216.1 2.7 reduce_sum.159
  218.8 0.0 copy-start.16
  218.9 32.0 %shard_map.103 = (bf16[8,512,128]{2,1,0:T(8,128)(2,1)S(1)}, bf16[8,64,128]{2,1,0:T(8,128)(2,1)S(1)}, f32[8,8,128]{2,1,0:T(8,128)S(1)}) custom-call(bf16[8,512,128]{2,1,0:T(8,128)(2,1)S(1)} %bitcast.104, bf16[8,64,128]{2,1,0:T(8,128)(2,1)S(1)} %bitcast.112, f32[8,8,128]{2,1,0:T(8,128)S(1)} %bitcast.119), custom_call_target="tpu_custom_call" | custom-call | tf_op jit(solution)/shard_map/pallas_call | solution.py:350
  251.0 0.1 multiply_convert_fusion.2.refs_0_
  251.1 12.4 %shard_map.104 = (bf16[16,64,128]{2,1,0:T(8,128)(2,1)S(1)}, f32[16,8,128]{2,1,0:T(8,128)S(1)}) custom-call(bf16[64,128]{1,0:T(8,128)(2,1)S(1)} %multiply_convert_fusion.2.refs_0_, f32[8,128]{1,0:T(8,128)S(1)} %broadcast_in_dim.27.refs_1_), custom_call_target="tpu_custom_call" | custom-call | tf_op jit(solution)/shard_map/pallas_call | solution.py:350
  263.6 0.1 mul.104
  263.7 0.1 dynamic_slice.17
  263.7 0.1 convert_reduce_fusion
  263.9 0.1 multiply_convert_fusion.1
  264.1 0.1 constant_dynamic-slice_fusion
  264.1 0.1 broadcast_bitcast_fusion
  264.3 0.2 subtract_add_fusion
  264.5 1.1 select_reduce_fusion
  265.6 0.6 compare_and_fusion
  266.2 0.8 fusion.38
  267.0 0.5 fusion.8
  267.5 0.8 fusion.37
  268.3 0.5 fusion.9
  268.8 1.1 multiply_convert_fusion
  270.0 0.6 convolution_dynamic-update-slice_fusion
  270.7 0.0 copy-start.15
  270.7 0.6 multiply_reduce_fusion.1
  271.3 33.7 %shard_map.105 = (bf16[8,512,128]{2,1,0:T(8,128)(2,1)S(1)}, bf16[8,128,128]{2,1,0:T(8,128)(2,1)S(1)}, f32[8,4,128]{2,1,0:T(4,128)S(1)}) custom-call(bf16[512,128]{1,0:T(8,128)(2,1)S(1)} %get-tuple-element.50.refs_0_, bf16[8,128,128]{2,1,0:T(8,128)(2,1)S(1)} %bitcast.111, f32[4,128]{1,0:T(4,128)S(1)} %bitcast.124), custom_call_target="tpu_custom_call" | custom-call | tf_op jit(solution)/shard_map/pallas_call | solution.py:350
  305.0 2.9 shard_map.106
  307.9 1.3 copy-done.11
  309.3 8.3 %shard_map.107 = bf16[16,64,128]{2,1,0:T(8,128)(2,1)S(1)} custom-call(bf16[64,128]{1,0:T(8,128)(2,1)S(1)} %reduce_sum.170.refs_0_), custom_call_target="tpu_custom_call" | custom-call | tf_op jit(solution)/shard_map/pallas_call | solution.py:350
  317.6 0.2 multiply_reduce_fusion
  317.8 0.1 reduce_sum.173
  317.9 0.6 reshape.208
  318.5 0.9 reduce_sum.171
  319.4 0.4 fusion.40
  319.9 0.2 copy-done.12
  320.1 3.7 %fusion.10 = bf16[1024,512,1]{1,0,2:T(8,128)(2,1)} fusion(bf16[1024,512]{1,0:T(8,128)(2,1)} %copy-done.13, f32[1024,512]{1,0:T(8,128)S(1)} %fusion.40, bf16[8,1024,128]{2,1,0:T(8,128)(2,1)S(1)} %bitcast.125, f32[1024]{0:T(1024)S(1)} %multiply_multiply_fusion, f32[1024]{0:T(1024)S(1)} %mul.104, f32[512]{0:T(512)S(1)} %convert_element_type.81, ...), kind=kOutput, calls=%fused_computation.26 | convolution fusion | flops 1077411840 | bytes 7350272 | tf_op jit(solution)/shard_map/hte,dhe->td/dot_general | solution.py:521
  323.8 14.7 %fusion.6 = bf16[1024,1,32]{2,1,0:T(2,128)(2,1)S(1)} fusion(bf16[1024,32,512]{2,1,0:T(8,128)(2,1)} %bitcast.127, bf16[1024,512,1]{1,0,2:T(8,128)(2,1)} %fusion.10), kind=kOutput, calls=%fused_computation.13 | convolution fusion | flops 33554432 | bytes 34668544 | tf_op jit(solution)/shard_map/bc,bkc->bk/dot_general | solution.py:529
  338.4 0.3 copy.46
  338.7 0.1 reshape.209
  338.9 0.2 copy.40
  339.1 0.2 reshape_reshape.31.refs_0_
  339.3 9.2 %shard_map.108 = bf16[16,32,128]{2,1,0:T(8,128)(2,1)S(1)} custom-call(bf16[8,32,128]{2,1,0:T(8,128)(2,1)S(1)} %reshape_reshape.31.refs_0_), custom_call_target="tpu_custom_call" | custom-call | tf_op jit(solution)/shard_map/pallas_call | solution.py:350
  348.5 0.1 reshape.210
  348.6 0.7 copy.41
  (54 shorter events, 0.5 us)
Async XLA Ops:
  0.0 206.7 %copy-start = (bf16[512,1024]{1,0:T(8,128)(2,1)S(1)}, bf16[512,1024]{1,0:T(8,128)(2,1)}, u32[]{:S(2)}) copy-start(bf16[512,1024]{1,0:T(8,128)(2,1)} %param.15) | copy-start | bytes 3145732
  2.6 0.9 copy-start.8
  20.3 0.6 copy-start.6
  192.9 13.1 %copy-start.17 = (bf16[512]{0:T(512)(128)(2,1)S(1)}, bf16[512]{0:T(512)(128)(2,1)}, u32[]{:S(2)}) copy-start(bf16[512]{0:T(512)(128)(2,1)} %param.13) | copy-start | bytes 3076
  206.0 0.7 copy-start.18
  206.3 1.6 copy-start.13
  206.7 1.3 copy-start.14
  208.5 0.9 copy-start.7
  212.7 1.3 copy-start.1
  214.0 0.7 copy-start.2
  214.7 0.7 copy-start.4
  215.4 0.6 copy-start.9
  216.1 2.7 copy-start.5
  216.1 2.8 copy-start.10
  218.8 45.3 %copy-start.16 = (s32[8,3]{0,1:T(4,128)S(1)}, s32[8,3]{0,1:T(4,128)}, u32[]{:S(2)}) copy-start(s32[8,3]{0,1:T(4,128)} %param.19) | copy-start | bytes 292
  266.2 1.3 copy-start.3
  270.7 48.8 %copy-start.15 = (bf16[512,128]{1,0:T(8,128)(2,1)S(1)}, bf16[512,128]{1,0:T(8,128)(2,1)}, u32[]{:S(2)}) copy-start(bf16[512,128]{1,0:T(8,128)(2,1)} %param.16) | copy-start | bytes 393220
  307.9 1.3 copy-start.11
  318.5 1.6 copy-start.12

commit v4 on v3

--- a/solution.py
+++ b/solution.py
@@ -23,6 +23,7 @@
 PAIR_BLOCK = 2048
 CONVERT_ROWS = 256
 UNROLL = 32
+INNER = 2
 
 
 def gather_kernel(idx_ref, block_ref, out_ref, table, picked):
@@ -283,11 +284,21 @@
     sources, results = refs[:count], refs[count : 2 * count]
     send_sem, recv_sem, local_sem = refs[2 * count :]
     peers = math.prod(lanes_of)
-    me = lax.axis_index(axes[0])
+    seq_index = lax.axis_index("seq")
+    if axes[0] == "seq_outer":
+        me = seq_index // INNER
+    elif axes[0] == "seq_inner":
+        me = lax.rem(seq_index, INNER)
+    else:
+        me = lax.axis_index(axes[0])
     if len(axes) > 1:
         me = me * lanes_of[1] + lax.axis_index(axes[1])
 
     def device(peer):
+        if axes[0] == "seq_outer":
+            return {"seq": peer * INNER + lax.rem(seq_index, INNER)}
+        if axes[0] == "seq_inner":
+            return {"seq": seq_index // INNER * INNER + peer}
         if len(axes) > 1:
             return {axes[0]: peer // lanes_of[1], axes[1]: lax.rem(peer, lanes_of[1])}
         return {axes[0]: peer}
@@ -340,7 +351,8 @@
 def exchange(axes, collective_id, *items):
     kinds = [kind for kind, _ in items]
     arrays = [array for _, array in items]
-    sizes = [lax.axis_size(axis) for axis in axes]
+    extent = {"seq_inner": INNER, "seq_outer": lax.axis_size("seq") // INNER}
+    sizes = [extent[axis] if axis in extent else lax.axis_size(axis) for axis in axes]
     peers = math.prod(sizes)
     shapes = [
         jax.ShapeDtypeStruct((peers,) + (a.shape if kind == "gather" else a.shape[1:]), a.dtype)
@@ -388,7 +400,7 @@
     heads_here = orig_queries.shape[0]
     tok_rows, top_count = codes_idx.shape
     ranges = seq_count // heads_here
-    if features % LANES or ranges != lat_count:
+    if features % LANES or ranges != lat_count or seq_count % INNER:
         return local_any(
             codes_idx,
             codes_val,
@@ -459,12 +471,25 @@
     def pair_sum(array):
         return jnp.sum(array.astype(jnp.float32), axis=0).astype(array.dtype)
 
+    outer = seq_count // INNER
+
+    def inner_first(array, *shape):
+        cut = array.reshape(outer, INNER, *shape)
+        return jnp.swapaxes(cut, 0, 1).reshape(INNER, -1, shape[-1])
+
     query_parts, key_parts, square_parts = exchange(
-        ("seq",),
+        ("seq_inner",),
         6,
-        ("scatter", pair_sum(query_pair).reshape(seq_count, range_len, head_dim)),
-        ("scatter", pair_sum(key_pair).reshape(seq_count, sub, head_dim)),
-        ("scatter", pair_sum(square_pair).reshape(seq_count, 8, LANES)),
+        ("scatter", inner_first(pair_sum(query_pair), range_len, head_dim)),
+        ("scatter", inner_first(pair_sum(key_pair), sub, head_dim)),
+        ("scatter", inner_first(pair_sum(square_pair), 8, LANES)),
+    )
+    query_parts, key_parts, square_parts = exchange(
+        ("seq_outer",),
+        8,
+        ("scatter", pair_sum(query_parts).reshape(outer, range_len, head_dim)),
+        ("scatter", pair_sum(key_parts).reshape(outer, sub, head_dim)),
+        ("scatter", pair_sum(square_parts).reshape(outer, 8, LANES)),
     )
     query_raw = jnp.sum(query_parts.astype(jnp.float32), axis=0)
     key_raw = jnp.sum(key_parts.astype(jnp.float32), axis=0)
@@ -498,11 +523,18 @@
     )[range_len:]
     query_inner = jnp.sum(query_grad.astype(jnp.float32) * query_new.astype(jnp.float32), axis=1)
     query_grads, key_grad_parts, inner_parts = exchange(
-        ("seq",),
+        ("seq_inner",),
         3,
         ("gather", query_grad),
-        ("scatter", by_token(key_grad.astype(jnp.bfloat16)).reshape(seq_count, tok_rows, head_dim)),
+        ("scatter", inner_first(by_token(key_grad.astype(jnp.bfloat16)), tok_rows, head_dim)),
         ("gather", query_inner.reshape(range_len // LANES, LANES)),
+    )
+    query_grads, key_grad_parts, inner_parts = exchange(
+        ("seq_outer",),
+        9,
+        ("gather", query_grads.reshape(-1, head_dim)),
+        ("scatter", pair_sum(key_grad_parts).reshape(outer, tok_rows, head_dim)),
+        ("gather", inner_parts.reshape(-1, LANES)),
     )
     query_grads, key_grad_pair, inner_parts = exchange(
         ("lat",),

time: 350 us -> 360 us (1.029)
  Pallas kernels: 289 us -> 294 us
    pallas_call x8 -> x10, Pallas kernels: 119 us -> 124 us  [exchange(): pl.pallas_call(functools.partial(exchange_kernel, axes, sizes, count, kin...]
    unnamed x42 -> x44, local copies, waits for them, and re-layouts: 9.33 us -> 9.91 us
where the time goes in v4:
time: 360 us
  Pallas kernels  294 us (82%)
  matrix products  37 us (10%)
  local copies, waits for them, and re-layouts  15.9 us (4%)
  other arithmetic  11.7 us (3%)
    pallas_call x1, Pallas kernels, gather_rows(): pl.pallas_call(gather_kernel, out_shape=jax.ShapeDtypeStruct((pairs, feat...  171 us
    pallas_call x10, Pallas kernels, exchange(): pl.pallas_call(functools.partial(exchange_kernel, axes, sizes, count, kin...  124 us
    dot_general x1, matrix products, local(): jnp.einsum('bc,bkc->bk', resid_grad, picked_rows, preferred_element_type=...  14.7 us
    dot_general x1, matrix products, local(): jnp.einsum('bk,bkc->bc', val_all, picked_rows, preferred_element_type=jnp...  13 us
    unnamed x44, local copies, waits for them, and re-layouts  9.91 us

profile of v4, /device:TPU:0, one launch (start us, length us, event | category | flops | bytes accessed | tf_op | source)
XLA Modules:
  0.0 359.6 jit_solution(1411869529875393778)
XLA Ops:
  0.0 0.8 constant_dynamic-slice_fusion.1.refs_3_
  0.8 0.8 copy.50
  1.6 0.1 reshape.215.refs_0_
  1.7 0.8 copy.51
  2.5 0.1 reshape.216.refs_1_
  2.6 0.9 copy-done.8
  3.5 16.7 %shard_map.100 = (s32[8,32,128]{2,1,0:T(8,128)S(1)}, bf16[8,32,128]{2,1,0:T(8,128)(2,1)S(1)}, bf16[8,64,128]{2,1,0:T(8,128)(2,1)S(1)}, bf16[8,64,128]{2,1,0:T(8,128)(2,1)S(1)}) custom-call(s32[32,128]{1,0:T(8,128)S(1)} %reshape.215.refs_0_, bf16[32,128]{1,0:T(8,128)(2,1)S(1)} %reshape.216.refs_1_, bf16[8,64,128]{2,1,0:T(8,128)(2,1)S(1)} %bitcast.144, ...), custom_call_target="tpu_custom_call" | custom-call | tf_op jit(solution)/shard_map/pallas_call | solution.py:362
  20.3 0.6 copy-done.5
  20.9 0.1 fusion.19.idx_ref
  21.0 170.9 %shard_map.101 = bf16[32768,512]{1,0:T(8,128)(2,1)} custom-call(s32[32768]{0:T(1024)S(1)} %fusion.19.idx_ref, bf16[16384,2048]{1,0:T(8,128)(2,1)} %bitcast.7.block_ref), custom_call_target="tpu_custom_call" | custom-call | tf_op jit(solution)/shard_map/pallas_call | solution.py:75
  191.9 1.0 reshape.258
  192.9 13.0 %fusion.39 = f32[1024,1,512]{2,1,0:T(1,128)S(1)} fusion(bf16[1024,32,1]{1,2,0:T(2,128)(2,1)} %reshape.258, bf16[1024,32,512]{2,1,0:T(8,128)(2,1)} %bitcast.152), kind=kOutput, calls=%fused_computation.94 | convolution fusion | flops 33554432 | bytes 35717120 | tf_op jit(solution)/shard_map/bk,bkc->bc/dot_general | solution.py:451
  206.0 0.3 fusion.1
  206.3 0.3 copy-done.19
  206.7 1.3 convolution_convert_fusion
  207.9 1.1 convolution_convert_fusion.1
  209.2 0.9 copy-done.2
  210.1 3.3 shard_map.102
  213.5 1.3 copy-done.1
  214.8 0.7 copy-done.3
  215.5 0.6 copy-done.9
  216.1 3.3 reduce_sum.204
  219.4 1.3 copy.55
  220.9 16.3 %shard_map.103 = (bf16[2,2048,128]{2,1,0:T(8,128)(2,1)S(1)}, bf16[2,256,128]{2,1,0:T(8,128)(2,1)S(1)}, f32[2,32,128]{2,1,0:T(8,128)S(1)}) custom-call(bf16[2,2048,128]{2,1,0:T(8,128)(2,1)S(1)} %bitcast.124, bf16[2,256,128]{2,1,0:T(8,128)(2,1)S(1)} %bitcast.133, f32[2,32,128]{2,1,0:T(8,128)S(1)} %bitcast.143), custom_call_target="tpu_custom_call" | custom-call | tf_op jit(solution)/shard_map/pallas_call | solution.py:362
  237.2 0.6 copy-done.7
  237.9 0.6 copy-done.11
  238.5 0.5 reduce_sum.207
  239.0 0.9 reduce_sum.208
  239.9 0.8 reduce_sum.209
  240.7 16.7 %shard_map.104 = (bf16[4,512,128]{2,1,0:T(8,128)(2,1)S(1)}, bf16[4,64,128]{2,1,0:T(8,128)(2,1)S(1)}, f32[4,8,128]{2,1,0:T(8,128)S(1)}) custom-call(bf16[4,512,128]{2,1,0:T(8,128)(2,1)S(1)} %bitcast.128, bf16[4,64,128]{2,1,0:T(8,128)(2,1)S(1)} %bitcast.137, f32[4,8,128]{2,1,0:T(8,128)S(1)} %bitcast.146), custom_call_target="tpu_custom_call" | custom-call | tf_op jit(solution)/shard_map/pallas_call | solution.py:362
  257.4 0.1 multiply_convert_fusion.2.refs_0_
  257.5 12.5 %shard_map.105 = (bf16[16,64,128]{2,1,0:T(8,128)(2,1)S(1)}, f32[16,8,128]{2,1,0:T(8,128)S(1)}) custom-call(bf16[64,128]{1,0:T(8,128)(2,1)S(1)} %multiply_convert_fusion.2.refs_0_, f32[8,128]{1,0:T(8,128)S(1)} %broadcast_in_dim.27.refs_1_), custom_call_target="tpu_custom_call" | custom-call | tf_op jit(solution)/shard_map/pallas_call | solution.py:362
  270.2 0.1 dynamic_slice.17
  270.3 0.1 multiply_convert_fusion.1
  270.5 0.1 constant_dynamic-slice_fusion
  270.7 0.2 subtract_add_fusion
  270.9 1.1 select_reduce_fusion
  272.1 0.6 compare_and_fusion
  272.7 0.8 fusion.38
  273.4 0.5 fusion.8
  274.0 0.8 fusion.37
  274.7 0.5 fusion.9
  275.3 1.1 multiply_convert_fusion
  276.4 0.6 convolution_dynamic-update-slice_fusion
  277.1 0.6 multiply_reduce_fusion.1
  277.7 8.7 %shard_map.106 = (bf16[2,512,128]{2,1,0:T(8,128)(2,1)S(1)}, bf16[2,512,128]{2,1,0:T(8,128)(2,1)S(1)}, f32[2,4,128]{2,1,0:T(4,128)S(1)}) custom-call(bf16[512,128]{1,0:T(8,128)(2,1)S(1)} %get-tuple-element.62.refs_0_, bf16[2,512,128]{2,1,0:T(8,128)(2,1)S(1)} %bitcast.132, f32[4,128]{1,0:T(4,128)S(1)} %bitcast.150), custom_call_target="tpu_custom_call" | custom-call | tf_op jit(solution)/shard_map/pallas_call | solution.py:362
  286.5 29.0 %shard_map.107 = (bf16[4,1024,128]{2,1,0:T(8,128)(2,1)S(1)}, bf16[4,128,128]{2,1,0:T(8,128)(2,1)S(1)}, f32[4,8,128]{2,1,0:T(8,128)S(1)}) custom-call(bf16[1024,128]{1,0:T(8,128)(2,1)S(1)} %bitcast.139, bf16[4,128,128]{2,1,0:T(8,128)(2,1)S(1)} %bitcast.134, f32[8,128]{1,0:T(8,128)S(1)} %bitcast.149), custom_call_target="tpu_custom_call" | custom-call | tf_op jit(solution)/shard_map/pallas_call | solution.py:362
  315.5 2.9 shard_map.108
  318.4 1.3 copy-done.12
  319.7 8.2 %shard_map.109 = bf16[16,64,128]{2,1,0:T(8,128)(2,1)S(1)} custom-call(bf16[64,128]{1,0:T(8,128)(2,1)S(1)} %reduce_sum.219.refs_0_), custom_call_target="tpu_custom_call" | custom-call | tf_op jit(solution)/shard_map/pallas_call | solution.py:362
  327.9 0.2 multiply_reduce_fusion
  328.2 0.6 reshape.248
  328.8 0.9 reduce_sum.220
  329.8 0.4 fusion.40
  330.2 0.2 copy-done.13
  330.4 3.7 %fusion.10 = bf16[1024,512,1]{1,0,2:T(8,128)(2,1)} fusion(bf16[1024,512]{1,0:T(8,128)(2,1)} %copy-done.14, f32[1024,512]{1,0:T(8,128)S(1)} %fusion.40, bf16[8,1024,128]{2,1,0:T(8,128)(2,1)S(1)} %bitcast.151, f32[1024]{0:T(1024)S(1)} %multiply_multiply_fusion, f32[1024]{0:T(1024)S(1)} %mul.104, f32[512]{0:T(512)S(1)} %convert_element_type.87, ...), kind=kOutput, calls=%fused_computation.25 | convolution fusion | flops 1077411840 | bytes 7350272 | tf_op jit(solution)/shard_map/hte,dhe->td/dot_general | solution.py:553
  334.1 14.7 %fusion.6 = bf16[1024,1,32]{2,1,0:T(2,128)(2,1)S(1)} fusion(bf16[1024,32,512]{2,1,0:T(8,128)(2,1)} %bitcast.153, bf16[1024,512,1]{1,0,2:T(8,128)(2,1)} %fusion.10), kind=kOutput, calls=%fused_computation.13 | convolution fusion | flops 33554432 | bytes 34668544 | tf_op jit(solution)/shard_map/bc,bkc->bk/dot_general | solution.py:561
  348.8 0.3 copy.71
  349.1 0.1 reshape.249
  349.2 0.2 copy.65
  349.4 0.2 reshape_reshape.31.refs_0_
  349.6 9.2 %shard_map.110 = bf16[16,32,128]{2,1,0:T(8,128)(2,1)S(1)} custom-call(bf16[8,32,128]{2,1,0:T(8,128)(2,1)S(1)} %reshape_reshape.31.refs_0_), custom_call_target="tpu_custom_call" | custom-call | tf_op jit(solution)/shard_map/pallas_call | solution.py:362
  358.8 0.1 reshape.250
  358.9 0.7 copy.66
  (66 shorter events, 0.9 us)
Async XLA Ops:
  0.0 206.7 %copy-start = (bf16[512,1024]{1,0:T(8,128)(2,1)S(1)}, bf16[512,1024]{1,0:T(8,128)(2,1)}, u32[]{:S(2)}) copy-start(bf16[512,1024]{1,0:T(8,128)(2,1)} %param.15) | copy-start | bytes 3145732
  2.6 0.9 copy-start.8
  20.3 0.6 copy-start.5
  192.9 13.1 %copy-start.18 = (bf16[512]{0:T(512)(128)(2,1)S(1)}, bf16[512]{0:T(512)(128)(2,1)}, u32[]{:S(2)}) copy-start(bf16[512]{0:T(512)(128)(2,1)} %param.13) | copy-start | bytes 3076
  206.0 0.7 copy-start.19
  206.3 1.6 copy-start.14
  206.7 1.3 copy-start.15
  209.2 0.9 copy-start.2
  213.5 1.3 copy-start.1
  214.8 0.7 copy-start.3
  215.5 0.6 copy-start.9
  216.1 4.6 %copy-start.4 = (bf16[2,512,128]{2,1,0:T(8,128)(2,1)S(1)}, bf16[2,512,128]{2,1,0:T(8,128)(2,1)}, u32[]{:S(2)}) copy-start(bf16[2,512,128]{2,1,0:T(8,128)(2,1)} %copy-done.3) | copy-start | bytes 786436
  219.4 1.4 copy-start.10
  237.2 0.6 copy-start.7
  237.9 0.6 copy-start.11
  238.5 32.0 %copy-start.17 = (s32[8,3]{0,1:T(4,128)S(1)}, s32[8,3]{0,1:T(4,128)}, u32[]{:S(2)}) copy-start(s32[8,3]{0,1:T(4,128)} %param.19) | copy-start | bytes 292
  272.6 1.3 copy-start.6
  277.7 52.0 %copy-start.16 = (bf16[512,128]{1,0:T(8,128)(2,1)S(1)}, bf16[512,128]{1,0:T(8,128)(2,1)}, u32[]{:S(2)}) copy-start(bf16[512,128]{1,0:T(8,128)(2,1)} %param.16) | copy-start | bytes 393220
  318.4 1.3 copy-start.12
  328.8 1.6 copy-start.13
